TPU v7x, 32 devices: a whole 2x2x4 slice. The times are simulated.
32 devices in a mesh: dp: 2 (over y), expert: 16 (over z, x, core).
Axes of the slice: x: 2, y: 2, z: 4, core: 2. Of those that a mesh axis runs over, the one named last changes fastest.
Arguments:
- out_grad: bfloat16 [512, 4096], P(('dp', 'expert')), may hold values from -6 to 6
- hidden_acts: bfloat16 [512, 8, 768], P(('dp', 'expert')), may hold values from -0.23925781 to 0.23925781
- gate_weights: float32 [512, 8], P(('dp', 'expert')), may hold values from 0 to 1, as said below
- expert_idx: int32 [512, 8], P(('dp', 'expert')), may hold values from 0 to 15, all different within a row; in each aligned block of 16 rows (0 to 15, 16 to 31, ...) at most 12 rows name the same one
- down_weight: bfloat16 [16, 768, 4096], P('expert'), may hold values from -0.09375 to 0.09375
Outputs:
- act_grad: bfloat16 [512, 8, 768], P(('dp', 'expert'))
- logit_grad: float32 [512, 8], P(('dp', 'expert'))
- down_grad: bfloat16 [16, 768, 4096], P('expert', 'dp')
Inputs may be any that keep to these rules, and one draw needn't show every extreme that they name: `expert_idx`: each row names 8 different experts; among the 16 rows of one device no expert is named more than 12 times, a bound that some block reaches. `gate_weights`: each row is positive and sums to one.
All inputs are finite; a program needn't handle non-finite values.
Results may differ from a plain program's by a relative error of at most 0.022.
Values may be sent and summed in bfloat16 or wider, within the bound.
A program may use at most 64 MiB of HBM per device.

v0:
```python
import jax
import jax.numpy as jnp
from jax import lax
from jax.sharding import PartitionSpec as P


def shards(out_grad, hidden_acts, gate_weights, expert_idx, down_weight):
    tok_rows, top_count = expert_idx.shape
    routed = tok_rows * top_count
    hidden_width = hidden_acts.shape[2]
    owners = lax.axis_size("expert")
    experts = owners * down_weight.shape[0]
    capacity = min(tok_rows, max(2, (3 * tok_rows * top_count + 2 * experts - 1) // (2 * experts)))
    slot_count = experts * capacity
    flat_expert = expert_idx.reshape(routed)
    member = (flat_expert[:, None] == jnp.arange(experts, dtype=jnp.int32)[None, :]).astype(
        jnp.bfloat16
    )
    row_line = jnp.arange(routed, dtype=jnp.int32)
    earlier_mask = (row_line[:, None] > row_line[None, :]).astype(jnp.bfloat16)
    earlier = jnp.dot(earlier_mask, member, preferred_element_type=jnp.float32)
    position = jnp.sum(earlier * member.astype(jnp.float32), axis=1).astype(jnp.int32)
    slot_index = flat_expert * capacity + position
    placement = (jnp.arange(slot_count, dtype=jnp.int32)[:, None] == slot_index[None, :]).astype(
        jnp.bfloat16
    )
    token_place = jnp.sum(placement.reshape(slot_count, tok_rows, top_count), axis=2)
    gate_half = lax.optimization_barrier(gate_weights.astype(jnp.bfloat16))
    send_grads = jnp.dot(token_place, out_grad, preferred_element_type=jnp.float32).astype(
        jnp.bfloat16
    )
    send_acts = jnp.dot(
        placement, hidden_acts.reshape(routed, hidden_width), preferred_element_type=jnp.float32
    ).astype(jnp.bfloat16)
    send_gate = jnp.dot(
        placement, gate_half.reshape(routed, 1), preferred_element_type=jnp.float32
    ).astype(jnp.bfloat16)
    grads_in, acts_in, gate_in = (
        lax.all_to_all(
            send_grads.reshape(owners, capacity, out_grad.shape[1]),
            "expert",
            split_axis=0,
            concat_axis=0,
            tiled=True,
        ),
        lax.all_to_all(
            send_acts.reshape(owners, capacity, hidden_width),
            "expert",
            split_axis=0,
            concat_axis=0,
            tiled=True,
        ),
        lax.all_to_all(
            send_gate.reshape(owners, capacity), "expert", split_axis=0, concat_axis=0, tiled=True
        ),
    )
    grads_in = grads_in.reshape(slot_count, out_grad.shape[1])
    acts_in = acts_in.reshape(slot_count, hidden_width)
    gate_rows = gate_in.reshape(slot_count, 1).astype(jnp.float32)
    expert_weight = down_weight[0]
    grad_hidden = lax.dot_general(
        grads_in, expert_weight, (((1,), (1,)), ((), ())), preferred_element_type=jnp.float32
    )
    act_back = (gate_rows * grad_hidden).astype(jnp.bfloat16)
    score_back = jnp.sum(grad_hidden * acts_in.astype(jnp.float32), axis=1).astype(jnp.bfloat16)
    scaled_grad = (gate_rows * grads_in.astype(jnp.float32)).astype(jnp.bfloat16)
    back_rows, back_scores = (
        lax.all_to_all(
            act_back.reshape(owners, capacity, hidden_width),
            "expert",
            split_axis=0,
            concat_axis=0,
            tiled=True,
        ),
        lax.all_to_all(
            score_back.reshape(owners, capacity), "expert", split_axis=0, concat_axis=0, tiled=True
        ),
    )
    weight_term = lax.dot_general(
        acts_in, scaled_grad, (((0,), (0,)), ((), ())), preferred_element_type=jnp.float32
    )
    summed = lax.psum_scatter(
        weight_term.astype(jnp.bfloat16), "dp", scatter_dimension=0, tiled=True
    )
    down_grad = summed[None]
    act_grad = lax.dot_general(
        placement,
        back_rows.reshape(slot_count, hidden_width),
        (((0,), (0,)), ((), ())),
        preferred_element_type=jnp.float32,
    ).astype(jnp.bfloat16)
    score_tok = lax.dot_general(
        placement,
        back_scores.reshape(slot_count, 1),
        (((0,), (0,)), ((), ())),
        preferred_element_type=jnp.float32,
    ).reshape(tok_rows, top_count)
    logit_grad = gate_weights * (
        score_tok - jnp.sum(gate_weights * score_tok, axis=1, keepdims=True)
    )
    return (act_grad.reshape(tok_rows, top_count, hidden_width), logit_grad, down_grad)


def solution(mesh):
    return jax.shard_map(
        shards,
        mesh=mesh,
        in_specs=(
            P(("dp", "expert"), None),
            P(("dp", "expert"), None, None),
            P(("dp", "expert"), None),
            P(("dp", "expert"), None),
            P("expert", None, None),
        ),
        out_specs=(
            P(("dp", "expert"), None, None),
            P(("dp", "expert"), None),
            P("expert", "dp", None),
        ),
        check_vma=False,
    )
```

profile of v0, /device:TPU:0, one launch (start us, length us, event | category | flops | bytes accessed | tf_op | source)
XLA Modules:
  0.0 179.4 jit_solution(14197340104337503663)
XLA Ops:
  7.2 0.7 convert_element_type.94
  7.9 0.1 copy.28
  8.0 0.1 reshape.149
  8.1 0.8 copy.27
  8.9 0.2 fusion.4
  9.1 0.2 fusion.10
  9.3 0.7 all_to_all.25
  10.0 7.4 %all-to-all-start = ((bf16[16,1,12]{2,1,0:T(2,128)(2,1)}), bf16[16,1,12]{2,1,0:T(2,128)(2,1)S(1)}, u32[]{:S(2)}, u32[]{:S(2)}) async-start(bf16[16,1,12]{2,1,0:T(2,128)(2,1)} %all_to_all.25), calls=%async_computation | async-start | bytes 16384 | tf_op jit(solution)/shard_map/all_to_all | solution.py:53
  17.4 0.2 convolution_convert_fusion.1
  17.7 0.8 reshape.144
  18.5 5.2 %all-to-all-done = bf16[16,1,12]{2,1,0:T(2,128)(2,1)S(1)} async-done(((bf16[16,1,12]{2,1,0:T(2,128)(2,1)}), bf16[16,1,12]{2,1,0:T(2,128)(2,1)S(1)}, u32[]{:S(2)}, u32[]{:S(2)}) %all-to-all-start) | async-done | bytes 416 | tf_op jit(solution)/shard_map/all_to_all | solution.py:53
  23.7 3.6 %all-to-all-start.3 = ((bf16[16,12,768]{2,1,0:T(8,128)(2,1)}), bf16[16,12,768]{2,1,0:T(8,128)(2,1)S(1)}, u32[]{:S(2)}, u32[]{:S(2)}) async-start(bf16[16,12,768]{2,1,0:T(8,128)(2,1)} %reshape.144), calls=%async_computation.3 | async-start | bytes 786432 | tf_op jit(solution)/shard_map/all_to_all | solution.py:46
  27.3 0.1 fusion.11
  27.4 1.5 convolution_convert_fusion
  28.9 1.5 reshape.138
  30.4 9.0 %all-to-all-done.3 = bf16[16,12,768]{2,1,0:T(8,128)(2,1)S(1)} async-done(((bf16[16,12,768]{2,1,0:T(8,128)(2,1)}), bf16[16,12,768]{2,1,0:T(8,128)(2,1)S(1)}, u32[]{:S(2)}, u32[]{:S(2)}) %all-to-all-start.3) | async-done | bytes 294944 | tf_op jit(solution)/shard_map/all_to_all | solution.py:46
  39.4 3.7 %all-to-all-start.1 = ((bf16[16,12,4096]{2,1,0:T(8,128)(2,1)}), bf16[16,12,4096]{2,1,0:T(8,128)(2,1)S(1)}, u32[]{:S(2)}, u32[]{:S(2)}) async-start(bf16[16,12,4096]{2,1,0:T(8,128)(2,1)} %reshape.138), calls=%async_computation.1 | async-start | bytes 4194304 | tf_op jit(solution)/shard_map/all_to_all | solution.py:39
  43.2 41.0 %all-to-all-done.1 = bf16[16,12,4096]{2,1,0:T(8,128)(2,1)S(1)} async-done(((bf16[16,12,4096]{2,1,0:T(8,128)(2,1)}), bf16[16,12,4096]{2,1,0:T(8,128)(2,1)S(1)}, u32[]{:S(2)}, u32[]{:S(2)}) %all-to-all-start.1) | async-done | bytes 1572896 | tf_op jit(solution)/shard_map/all_to_all | solution.py:39
  84.2 4.6 %bitcast_convert_fusion = bf16[768,4096]{1,0:T(8,128)(2,1)} fusion(bf16[16,12,768]{2,1,0:T(8,128)(2,1)S(1)} %all-to-all-done.3, bf16[16,12,4096]{2,1,0:T(8,128)(2,1)S(1)} %all-to-all-done.1, f32[16,12]{1,0:T(8,128)S(1)} %bitcast.32), kind=kOutput, calls=%fused_computation | convolution fusion | flops 1213464576 | bytes 8160000 | tf_op jit(solution)/shard_map/dot_general | solution.py:79
  89.0 1.3 reshape.139
  90.4 5.6 %multiply_reduce_fusion = (bf16[192]{0:T(256)(128)(2,1)S(1)}, bf16[192,768]{1,0:T(8,128)(2,1)S(1)}) fusion(f32[192,768]{1,0:T(8,128)S(1)} %reshape.147, f32[192]{0:T(256)S(1)} %reshape.146, bf16[192,4096]{1,0:T(8,128)(2,1)} %reshape.139, bf16[1,768,4096]{2,1,0:T(8,128)(2,1)} %param.9), kind=kOutput, calls=%fused_computation.11 | convolution fusion | flops 1208549120 | bytes 8750208 | tf_op jit(solution)/shard_map/dot_general | solution.py:61
  96.0 0.7 convert_element_type.116
  96.7 11.2 %all-to-all-start.4 = ((bf16[16,1,12]{2,1,0:T(2,128)(2,1)}), bf16[16,1,12]{2,1,0:T(2,128)(2,1)S(1)}, u32[]{:S(2)}, u32[]{:S(2)}) async-start(bf16[16,1,12]{2,1,0:T(2,128)(2,1)} %convert_element_type.116), calls=%async_computation.4 | async-start | bytes 16384 | tf_op jit(solution)/shard_map/all_to_all | solution.py:75
  107.9 0.8 reshape.140
  108.7 5.5 %all-to-all-done.4 = bf16[16,1,12]{2,1,0:T(2,128)(2,1)S(1)} async-done(((bf16[16,1,12]{2,1,0:T(2,128)(2,1)}), bf16[16,1,12]{2,1,0:T(2,128)(2,1)S(1)}, u32[]{:S(2)}, u32[]{:S(2)}) %all-to-all-start.4) | async-done | bytes 416 | tf_op jit(solution)/shard_map/all_to_all | solution.py:75
  114.2 3.6 %all-to-all-start.2 = ((bf16[16,12,768]{2,1,0:T(8,128)(2,1)}), bf16[16,12,768]{2,1,0:T(8,128)(2,1)S(1)}, u32[]{:S(2)}, u32[]{:S(2)}) async-start(bf16[16,12,768]{2,1,0:T(8,128)(2,1)} %reshape.140), calls=%async_computation.2 | async-start | bytes 786432 | tf_op jit(solution)/shard_map/all_to_all | solution.py:68
  117.8 0.1 reshape.151
  117.9 0.3 fusion.8
  118.3 0.6 fusion.18
  118.9 11.0 %all-to-all-done.2 = bf16[16,12,768]{2,1,0:T(8,128)(2,1)S(1)} async-done(((bf16[16,12,768]{2,1,0:T(8,128)(2,1)}), bf16[16,12,768]{2,1,0:T(8,128)(2,1)S(1)}, u32[]{:S(2)}, u32[]{:S(2)}) %all-to-all-start.2) | async-done | bytes 294944 | tf_op jit(solution)/shard_map/all_to_all | solution.py:68
  130.0 0.9 fusion.3
  130.9 41.6 %reduce-scatter.2.cloned.1.call-done = bf16[384,4096]{1,0:T(8,128)(2,1)} async-done(((bf16[768,4096]{1,0:T(8,128)(2,1)}), bf16[384,4096]{1,0:T(8,128)(2,1)}) %reduce-scatter.2.cloned.1.call-update) | async-done | bytes 3145744 | tf_op jit(solution)/shard_map/reduce_scatter | solution.py:82
  (20 shorter events, 0.7 us)
Async XLA Ops:
  7.2 10.2 %copy-start = (bf16[16,8,768]{2,1,0:T(8,128)(2,1)S(1)}, bf16[16,8,768]{2,1,0:T(8,128)(2,1)}, u32[]{:S(2)}) copy-start(bf16[16,8,768]{2,1,0:T(8,128)(2,1)} %param.6) | copy-start | bytes 589828
  10.0 13.7 %all-to-all-start = ((bf16[16,1,12]{2,1,0:T(2,128)(2,1)}), bf16[16,1,12]{2,1,0:T(2,128)(2,1)S(1)}, u32[]{:S(2)}, u32[]{:S(2)}) async-start(bf16[16,1,12]{2,1,0:T(2,128)(2,1)} %all_to_all.25), calls=%async_computation | async-start | bytes 16384 | tf_op jit(solution)/shard_map/all_to_all | solution.py:53
  23.7 15.7 %all-to-all-start.3 = ((bf16[16,12,768]{2,1,0:T(8,128)(2,1)}), bf16[16,12,768]{2,1,0:T(8,128)(2,1)S(1)}, u32[]{:S(2)}, u32[]{:S(2)}) async-start(bf16[16,12,768]{2,1,0:T(8,128)(2,1)} %reshape.144), calls=%async_computation.3 | async-start | bytes 786432 | tf_op jit(solution)/shard_map/all_to_all | solution.py:46
  39.4 44.8 %all-to-all-start.1 = ((bf16[16,12,4096]{2,1,0:T(8,128)(2,1)}), bf16[16,12,4096]{2,1,0:T(8,128)(2,1)S(1)}, u32[]{:S(2)}, u32[]{:S(2)}) async-start(bf16[16,12,4096]{2,1,0:T(8,128)(2,1)} %reshape.138), calls=%async_computation.1 | async-start | bytes 4194304 | tf_op jit(solution)/shard_map/all_to_all | solution.py:39
  43.2 129.4 %reduce-scatter.2.cloned.1.call-start = ((), (), s32[]{:S(2)}) async-start(), calls=%async_computation.6 | async-start | bytes 9437184 | tf_op jit(solution)/shard_map/reduce_scatter | solution.py:82
  90.4 27.9 %copy-start.1 = (f32[16,8]{0,1:T(8,128)S(1)}, f32[16,8]{0,1:T(8,128)}, u32[]{:S(2)}) copy-start(f32[16,8]{0,1:T(8,128)} %param.7) | copy-start | bytes 1540
  96.7 17.5 %all-to-all-start.4 = ((bf16[16,1,12]{2,1,0:T(2,128)(2,1)}), bf16[16,1,12]{2,1,0:T(2,128)(2,1)S(1)}, u32[]{:S(2)}, u32[]{:S(2)}) async-start(bf16[16,1,12]{2,1,0:T(2,128)(2,1)} %convert_element_type.116), calls=%async_computation.4 | async-start | bytes 16384 | tf_op jit(solution)/shard_map/all_to_all | solution.py:75
  114.2 15.7 %all-to-all-start.2 = ((bf16[16,12,768]{2,1,0:T(8,128)(2,1)}), bf16[16,12,768]{2,1,0:T(8,128)(2,1)S(1)}, u32[]{:S(2)}, u32[]{:S(2)}) async-start(bf16[16,12,768]{2,1,0:T(8,128)(2,1)} %reshape.140), calls=%async_computation.2 | async-start | bytes 786432 | tf_op jit(solution)/shard_map/all_to_all | solution.py:68
Sparse Core Ops, SparseCore 0:
  88.9 83.5 reduce-scatter.1
where the time goes:
time: 180 us; the launch traced here: 179 us
  waiting for transfers between devices  113 us (63%)
  starting transfers between devices  29.4 us (16%)
  between operations  14.2 us (8%)
  matrix products  13.5 us (8%)
  local copies, waits for them, and re-layouts  7.45 us (4%)
    reduce_scatter x1, waiting for transfers between devices, shards(): lax.psum_scatter(weight_term.astype(jnp.bfloat16), 'dp', scatter_dimensio...  41.6 us
    all_to_all x1, waiting for transfers between devices, shards(): lax.all_to_all(send_grads.reshape(owners, capacity, out_grad.shape[1]), '...  41 us
    all_to_all x1, starting transfers between devices, shards(): lax.all_to_all(score_back.reshape(owners, capacity), 'expert', split_axis...  11.2 us
    all_to_all x1, waiting for transfers between devices, shards(): lax.all_to_all(act_back.reshape(owners, capacity, hidden_width), 'expert'...  11 us
    all_to_all x1, waiting for transfers between devices, shards(): lax.all_to_all(send_acts.reshape(owners, capacity, hidden_width), 'expert...  9.01 us
    all_to_all x1, starting transfers between devices, shards(): lax.all_to_all(send_gate.reshape(owners, capacity), 'expert', split_axis=...  7.36 us
    dot_general x1, matrix products, shards(): lax.dot_general(grads_in, expert_weight, (((1,), (1,)), ((), ())), prefer...  5.6 us
    all_to_all x1, waiting for transfers between devices, shards(): lax.all_to_all(score_back.reshape(owners, capacity), 'expert', split_axis...  5.49 us
  transfers between devices with their start and end apart: 6, of which 6 were waited for; matrix products, arithmetic and copies ran while one was open for 8% of the time, Pallas kernels for 0%

commit v1 on v0

--- a/solution.py
+++ b/solution.py
@@ -1,10 +1,17 @@
+import functools
+
 import jax
 import jax.numpy as jnp
 from jax import lax
+from jax.experimental import pallas as pl
+from jax.experimental.pallas import tpu as pltpu
 from jax.sharding import PartitionSpec as P
 
-
-def shards(out_grad, hidden_acts, gate_weights, expert_idx, down_weight):
+MESH = pl.DeviceIdType.MESH
+ZS, XS, CS = 4, 2, 2
+
+
+def routed_shards(out_grad, hidden_acts, gate_weights, expert_idx, down_weight):
     tok_rows, top_count = expert_idx.shape
     routed = tok_rows * top_count
     hidden_width = hidden_acts.shape[2]
@@ -101,9 +108,360 @@
     return (act_grad.reshape(tok_rows, top_count, hidden_width), logit_grad, down_grad)
 
 
+def slot_of(y, x, z, c):
+    return y * (XS * ZS * CS) + x * (ZS * CS) + z * CS + c
+
+
+def expert_of(x, z, c):
+    return z * (XS * CS) + x * CS + c
+
+
+def gather_kernel(
+    gate_ref, idx_ref, acts_ref, grad_ref, w_hbm,
+    act_out, logit_out, down_out,
+    grads, w_buf, acts_send, acts_in, acts_t, hid, back,
+    w_sem, own_sem, g_recv, z_send, x_send, y_send, c_send,
+    h_send, h_recv, b_send, b_recv,
+):
+    y = lax.axis_index("dp")
+    me = lax.axis_index("expert")
+    z = lax.div(me, XS * CS)
+    x = lax.rem(lax.div(me, CS), XS)
+    c = lax.rem(me, CS)
+    n_exp = ZS * XS * CS
+    n_dev = 2 * n_exp
+    tok, top = idx_ref.shape
+    routed, width = acts_ref.shape
+    half = width // 2
+    model = grad_ref.shape[1]
+    lid = y * n_exp + me
+    own = slot_of(y, x, z, c)
+
+    def dev(yy, ee):
+        return {"dp": yy, "expert": ee}
+
+    barrier = pltpu.get_barrier_semaphore()
+
+    def greet(r, carry):
+        other = lax.rem(lid + r, n_dev)
+        pl.semaphore_signal(
+            barrier, inc=1,
+            device_id=dev(lax.div(other, n_exp), lax.rem(other, n_exp)),
+            device_id_type=MESH,
+        )
+        return carry
+
+    lax.fori_loop(1, n_dev, greet, 0)
+    w_copy = pltpu.make_async_copy(w_hbm, w_buf, w_sem)
+    w_copy.start()
+    own_grad = pltpu.make_async_copy(grad_ref, grads.at[own], own_sem.at[0])
+    own_grad.start()
+
+    gate = gate_ref[...]
+    gate_half = gate.astype(jnp.bfloat16).astype(jnp.float32)
+    idx = idx_ref[...].astype(jnp.float32)
+    lane = lax.broadcasted_iota(jnp.int32, (tok, routed), 1)
+    line = lax.broadcasted_iota(jnp.int32, (tok, routed), 0)
+    gate_wide = jnp.zeros((tok, routed), jnp.float32)
+    idx_wide = jnp.zeros((tok, routed), jnp.float32)
+    for k in range(top):
+        here = (lane == line * top + k)
+        gate_wide = jnp.where(here, gate_half[:, k:k + 1], gate_wide)
+        idx_wide = jnp.where(here, idx[:, k:k + 1], idx_wide)
+    gate_row = jnp.sum(gate_wide, axis=0, keepdims=True)
+    idx_row = jnp.sum(idx_wide, axis=0, keepdims=True)
+    rows = n_exp * tok
+    row = lax.broadcasted_iota(jnp.int32, (rows, routed), 0)
+    col = lax.broadcasted_iota(jnp.int32, (rows, routed), 1)
+    row_exp = lax.div(row, tok).astype(jnp.float32)
+    place = jnp.where(
+        (idx_row == row_exp) & (lax.div(col, top) == lax.rem(row, tok)), gate_row, 0.0
+    ).astype(jnp.bfloat16)
+    weighted = jnp.dot(place, acts_ref[...], preferred_element_type=jnp.float32)
+    weighted = weighted.astype(jnp.bfloat16).reshape(n_exp, tok, width)
+    acts_send[0] = weighted[:, :, :half]
+    acts_send[1] = weighted[:, :, half:]
+
+    pl.semaphore_wait(barrier, n_dev - 1)
+
+    def grad_copy(src, slot, sem, yy, ee):
+        return pltpu.make_async_remote_copy(
+            src_ref=src, dst_ref=grads.at[slot], send_sem=sem, recv_sem=g_recv.at[slot],
+            device_id=dev(yy, ee), device_id_type=MESH,
+        )
+
+    def arrived(slot):
+        grad_copy(grad_ref, slot, c_send.at[0], y, expert_of(x, z, 1 - c)).wait_recv()
+
+    sent = []
+
+    def send(copy, when=None):
+        if when is None:
+            copy.start()
+        else:
+            pl.when(when)(copy.start)
+        sent.append((when, copy))
+
+    def pass_on(src, yy, xx, zz, to_x, to_y, when=None):
+        slot = slot_of(yy, xx, zz, c)
+        in_plane = xx * ZS + zz
+        if to_x:
+            send(grad_copy(src, slot, x_send.at[zz], y, expert_of(1 - x, z, c)), when)
+        if to_y:
+            send(grad_copy(src, slot, y_send.at[in_plane], 1 - y, me), when)
+        send(
+            grad_copy(src, slot, c_send.at[yy * XS * ZS + in_plane], y, expert_of(x, z, 1 - c)),
+            when,
+        )
+
+    def along_z(src, zz, way, when):
+        slot = slot_of(y, x, zz, c)
+        send(
+            grad_copy(
+                src, slot, z_send.at[(way + 1) // 2, zz], y, expert_of(x, z + way, c)
+            ),
+            when,
+        )
+
+    for way in (1, -1):
+        along_z(grad_ref, z, way, (z + way >= 0) & (z + way < ZS))
+    pass_on(grad_ref, y, x, z, True, True)
+
+    def from_z(dist):
+        for way in (1, -1):
+            zz = z - way * dist
+            there = (zz >= 0) & (zz < ZS)
+            slot = slot_of(y, x, zz, c)
+            pl.when(there)(functools.partial(arrived, slot))
+            along_z(grads.at[slot], zz, way, there & (z + way >= 0) & (z + way < ZS))
+            pass_on(grads.at[slot], y, x, zz, True, True, there)
+
+    def from_x(dist):
+        for way in (1, -1) if dist else (1,):
+            zz = z - way * dist
+            there = (zz >= 0) & (zz < ZS) if dist else None
+            slot = slot_of(y, 1 - x, zz, c)
+            if dist:
+                pl.when(there)(functools.partial(arrived, slot))
+            else:
+                arrived(slot)
+            pass_on(grads.at[slot], y, 1 - x, zz, False, True, there)
+
+    def acts_copy(r):
+        other = lax.rem(lid + r, n_dev)
+        yy, ee = lax.div(other, n_exp), lax.rem(other, n_exp)
+        return pltpu.make_async_remote_copy(
+            src_ref=acts_send.at[yy, ee], dst_ref=acts_in.at[own],
+            send_sem=h_send.at[r], recv_sem=h_recv.at[own],
+            device_id=dev(yy, ee), device_id_type=MESH,
+        )
+
+    def acts_start(r, carry):
+        acts_copy(r).start()
+        return carry
+
+    own_acts = pltpu.make_async_copy(acts_send.at[y, me], acts_in.at[own], own_sem.at[1])
+
+    def back_copy(slot, zz, xx, cc):
+        return pltpu.make_async_remote_copy(
+            src_ref=hid.at[slot], dst_ref=back.at[me],
+            send_sem=b_send.at[slot], recv_sem=b_recv.at[me],
+            device_id=dev(y, expert_of(xx, zz, cc)), device_id_type=MESH,
+        )
+
+    per_x = ZS * CS
+    tile = 256
+
+    def hidden(xx):
+        lhs = grads[pl.ds(slot_of(y, xx, 0, 0), per_x)].reshape(per_x * tok, model)
+
+        @pl.loop(0, width // tile)
+        def _(n):
+            cols = pl.ds(pl.multiple_of(n * tile, tile), tile)
+            part = lax.dot_general(
+                lhs, w_buf[cols, :], (((1,), (1,)), ((), ())),
+                preferred_element_type=jnp.float32,
+            )
+            hid[pl.ds(xx * per_x, per_x), :, cols] = part.astype(jnp.bfloat16).reshape(
+                per_x, tok, tile
+            )
+
+    from_z(1)
+    from_x(0)
+    from_z(2)
+    from_x(1)
+    from_z(3)
+    lax.fori_loop(1, n_dev, acts_start, 0)
+    own_acts.start()
+    from_x(2)
+    own_grad.wait()
+    w_copy.wait()
+    for zz in range(ZS):
+        arrived(slot_of(y, x, zz, 1 - c))
+    hidden(x)
+    own_back = pltpu.make_async_copy(hid.at[own - y * n_exp], back.at[me], own_sem.at[2])
+    own_back.start()
+    for r in range(1, per_x):
+        at = lax.rem(z * CS + c + r, per_x)
+        back_copy(x * per_x + at, lax.div(at, CS), x, lax.rem(at, CS)).start()
+    from_x(3)
+    for zz in range(ZS):
+        arrived(slot_of(y, 1 - x, zz, 1 - c))
+    hidden(1 - x)
+    for r in range(per_x):
+        at = lax.rem(z * CS + c + r, per_x)
+        back_copy((1 - x) * per_x + at, lax.div(at, CS), 1 - x, lax.rem(at, CS)).start()
+
+    for xx in (x, 1 - x):
+        for zz in range(ZS):
+            slot = slot_of(1 - y, xx, zz, c)
+            arrived(slot)
+            pass_on(grads.at[slot], 1 - y, xx, zz, False, False)
+
+    def acts_wait(r, carry):
+        other = lax.rem(lid + r, n_dev)
+        yy, ee = lax.div(other, n_exp), lax.rem(other, n_exp)
+        slot = slot_of(
+            yy, lax.rem(lax.div(ee, CS), XS), lax.div(ee, XS * CS), lax.rem(ee, CS)
+        )
+        pltpu.make_async_remote_copy(
+            src_ref=acts_send.at[0, 0], dst_ref=acts_in.at[slot],
+            send_sem=h_send.at[r], recv_sem=h_recv.at[slot],
+            device_id=dev(yy, ee), device_id_type=MESH,
+        ).wait_recv()
+        return carry
+
+    lax.fori_loop(1, n_dev, acts_wait, 0)
+    own_acts.wait()
+    acts_t[...] = acts_in[...].reshape(n_dev * tok, half).T
+    for xx in range(XS):
+        for zz in range(ZS):
+            arrived(slot_of(1 - y, xx, zz, 1 - c))
+
+    @pl.loop(0, model // tile)
+    def _(n):
+        cols = pl.ds(pl.multiple_of(n * tile, tile), tile)
+        down_out[:, cols] = jnp.dot(
+            acts_t[...], grads[:, :, cols].reshape(n_dev * tok, tile),
+            preferred_element_type=jnp.float32,
+        ).astype(jnp.bfloat16)
+
+    def back_wait(r, carry):
+        ee = lax.rem(me + r, n_exp)
+        pltpu.make_async_remote_copy(
+            src_ref=hid.at[0], dst_ref=back.at[ee],
+            send_sem=b_send.at[0], recv_sem=b_recv.at[ee],
+            device_id=dev(y, ee), device_id_type=MESH,
+        ).wait_recv()
+        return carry
+
+    lax.fori_loop(1, n_exp, back_wait, 0)
+    own_back.wait()
+    tall_row = lax.broadcasted_iota(jnp.int32, (routed, tok), 0)
+    tall_col = lax.broadcasted_iota(jnp.int32, (routed, tok), 1)
+    spread = (lax.div(tall_row, top) == tall_col).astype(jnp.float32)
+    own_k = (
+        lax.broadcasted_iota(jnp.int32, (routed, top), 1)
+        == lax.rem(lax.broadcasted_iota(jnp.int32, (routed, top), 0), top)
+    ).astype(jnp.float32)
+    gate_col = jnp.sum(
+        jnp.dot(spread, gate_half, preferred_element_type=jnp.float32) * own_k,
+        axis=1, keepdims=True,
+    )
+    idx_col = jnp.sum(
+        jnp.dot(spread, idx, preferred_element_type=jnp.float32) * own_k, axis=1, keepdims=True
+    )
+    row = lax.broadcasted_iota(jnp.int32, (routed, rows), 0)
+    col = lax.broadcasted_iota(jnp.int32, (routed, rows), 1)
+    pick = (
+        (idx_col == lax.div(col, tok).astype(jnp.float32))
+        & (lax.div(row, top) == lax.rem(col, tok))
+    ).astype(jnp.float32).astype(jnp.bfloat16)
+    picked = jnp.dot(pick, back[...].reshape(rows, width), preferred_element_type=jnp.float32)
+    act_out[...] = (gate_col * picked).astype(jnp.bfloat16)
+    score = jnp.sum(picked * acts_ref[...].astype(jnp.float32), axis=1, keepdims=True)
+    score = score.astype(jnp.bfloat16).astype(jnp.float32)
+    gather = (
+        lax.div(lane, top) == line
+    ).astype(jnp.float32)
+    score = jnp.dot(gather, score * own_k, preferred_element_type=jnp.float32)
+    logit_out[...] = gate * (score - jnp.sum(gate * score, axis=1, keepdims=True))
+
+    for when, copy in sent:
+        if when is None:
+            copy.wait_send()
+        else:
+            pl.when(when)(copy.wait_send)
+
+    def acts_sent(r, carry):
+        acts_copy(r).wait_send()
+        return carry
+
+    lax.fori_loop(1, n_dev, acts_sent, 0)
+    for r in range(1, per_x):
+        at = lax.rem(z * CS + c + r, per_x)
+        back_copy(x * per_x + at, lax.div(at, CS), x, lax.rem(at, CS)).wait_send()
+    for r in range(per_x):
+        at = lax.rem(z * CS + c + r, per_x)
+        back_copy((1 - x) * per_x + at, lax.div(at, CS), 1 - x, lax.rem(at, CS)).wait_send()
+
+
+def gathered_shards(out_grad, hidden_acts, gate_weights, expert_idx, down_weight):
+    tok, top = expert_idx.shape
+    model = out_grad.shape[1]
+    width = hidden_acts.shape[2]
+    half = width // 2
+    n_exp = ZS * XS * CS
+    n_dev = 2 * n_exp
+    dma = pltpu.SemaphoreType.DMA
+    vmem = pl.BlockSpec(memory_space=pltpu.VMEM)
+    act, logit, down = pl.pallas_call(
+        gather_kernel,
+        out_shape=(
+            jax.ShapeDtypeStruct((tok * top, width), jnp.bfloat16),
+            jax.ShapeDtypeStruct((tok, top), jnp.float32),
+            jax.ShapeDtypeStruct((half, model), jnp.bfloat16),
+        ),
+        in_specs=[vmem] * 4 + [pl.BlockSpec(memory_space=pl.ANY)],
+        out_specs=(vmem, vmem, vmem),
+        scratch_shapes=[
+            pltpu.VMEM((n_dev, tok, model), jnp.bfloat16),
+            pltpu.VMEM((width, model), jnp.bfloat16),
+            pltpu.VMEM((2, n_exp, tok, half), jnp.bfloat16),
+            pltpu.VMEM((n_dev, tok, half), jnp.bfloat16),
+            pltpu.VMEM((half, n_dev * tok), jnp.bfloat16),
+            pltpu.VMEM((n_exp, tok, width), jnp.bfloat16),
+            pltpu.VMEM((n_exp, tok, width), jnp.bfloat16),
+            dma,
+            dma((3,)),
+            dma((n_dev,)),
+            dma((2, ZS)),
+            dma((ZS,)),
+            dma((XS * ZS,)),
+            dma((2 * XS * ZS,)),
+            dma((n_dev,)),
+            dma((n_dev,)),
+            dma((n_exp,)),
+            dma((n_exp,)),
+        ],
+        compiler_params=pltpu.CompilerParams(
+            collective_id=0, has_side_effects=True, vmem_limit_bytes=48 * 1024 * 1024
+        ),
+        cost_estimate=pl.CostEstimate(
+            flops=6 * n_exp * tok * model * width, bytes_accessed=3 * width * model * 2,
+            transcendentals=0,
+        ),
+    )(
+        gate_weights, expert_idx, hidden_acts.reshape(tok * top, width), out_grad,
+        down_weight.reshape(width, model),
+    )
+    return act.reshape(tok, top, width), logit, down[None]
+
+
 def solution(mesh):
+    gathered = mesh.shape["dp"] == 2 and mesh.shape["expert"] == ZS * XS * CS
     return jax.shard_map(
-        shards,
+        gathered_shards if gathered else routed_shards,
         mesh=mesh,
         in_specs=(
             P(("dp", "expert"), None),

time: 180 us -> 51.5 us (0.29)
  waiting for transfers between devices: 113 us -> 0 us
  Pallas kernels: 0 us -> 44.1 us
  starting transfers between devices: 29.4 us -> 0 us
  between operations: 14.2 us -> 0.64 us
  matrix products: 13.5 us -> 0 us
    all_to_all x5 -> x0, waiting for transfers between devices: 71.6 us -> none  [the longest x1 41 us: shards(): lax.all_to_all(send_grads.reshape(owners, capacity, out_grad.shape[1]), '...]
    pallas_call x0 -> x1, Pallas kernels: none -> 44.1 us  [gathered_shards(): pl.pallas_call(gather_kernel, out_shape=(jax.ShapeDtypeStruct((tok * top,...]
    reduce_scatter x1 -> x0, waiting for transfers between devices: 41.6 us -> none  [shards(): lax.psum_scatter(weight_term.astype(jnp.bfloat16), 'dp', scatter_dimensio...]
    all_to_all x5 -> x0, starting transfers between devices: 29.4 us -> none  [the longest x1 11.2 us: shards(): lax.all_to_all(score_back.reshape(owners, capacity), 'expert', split_axis...]
    dot_general x8 -> x0, matrix products: 13.5 us -> none  [the longest x1 5.6 us: shards(): lax.dot_general(grads_in, expert_weight, (((1,), (1,)), ((), ())), prefer...]
    unnamed x5 -> x9, local copies, waits for them, and re-layouts: 0.78 us -> 6.35 us
    reshape x7 -> x0, local copies, waits for them, and re-layouts: 4.76 us -> none  [the longest x1 1.51 us: shards(): send_grads.reshape(owners, capacity, out_grad.shape[1])]
  transfers between devices with their start and end apart: 6 -> 0, of which waited for: 6 -> 0; matrix products, arithmetic and copies ran while one was open for 8% -> 0% of each run, Pallas kernels for 0% -> 0%
where the time goes in v1:
time: 51.5 us; the launch traced here: 51 us
  Pallas kernels  44.1 us (86%)
  local copies, waits for them, and re-layouts  6.35 us (12%)
  between operations  0.64 us (1%)
    pallas_call x1, Pallas kernels, gathered_shards(): pl.pallas_call(gather_kernel, out_shape=(jax.ShapeDtypeStruct((tok * top,...  44.1 us
    unnamed x9, local copies, waits for them, and re-layouts  6.35 us

profile of v1, /device:TPU:0, one launch (start us, length us, event | category | flops | bytes accessed | tf_op | source)
XLA Modules:
  0.0 51.0 jit_solution(13718346119619991769)
XLA Ops:
  0.6 0.8 %copy.8.gate_ref = f32[16,8]{1,0:T(8,128)S(1)} copy(f32[16,8]{0,1:T(8,128)} %param.7) | data formatting | bytes 1024 | tf_op args[2]
  1.4 0.8 %copy.9.idx_ref = s32[16,8]{1,0:T(8,128)S(1)} copy(s32[16,8]{0,1:T(8,128)} %param.8) | data formatting | bytes 1024 | tf_op args[3]
  2.1 0.0 copy-start
  2.1 0.9 %copy-done = bf16[16,8,768]{2,1,0:T(8,128)(2,1)S(1)} copy-done((bf16[16,8,768]{2,1,0:T(8,128)(2,1)S(1)}, bf16[16,8,768]{2,1,0:T(8,128)(2,1)}, u32[]{:S(2)}) %copy-start) | copy-done | bytes 196632
  3.1 0.0 copy-start.1
  3.1 0.9 %copy-done.1 = bf16[16,4096]{1,0:T(8,128)(2,1)S(1)} copy-done((bf16[16,4096]{1,0:T(8,128)(2,1)S(1)}, bf16[16,4096]{1,0:T(8,128)(2,1)}, u32[]{:S(2)}) %copy-start.1) | copy-done | bytes 131096
  4.0 44.1 %shard_map.76 = (bf16[128,768]{1,0:T(8,128)(2,1)S(1)}, f32[16,8]{1,0:T(8,128)S(1)}, bf16[384,4096]{1,0:T(8,128)(2,1)S(1)}) custom-call(f32[16,8]{1,0:T(8,128)S(1)} %copy.8.gate_ref, s32[16,8]{1,0:T(8,128)S(1)} %copy.9.idx_ref, bf16[128,768]{1,0:T(8,128)(2,1)S(1)} %bitcast.6, bf16[16,4096]{1,0:T(8,128)(2,1)S(1)} %copy-done.1, bf16[768,4096]{1,0:T(8,128)(2,1)} %bitcast.7), custom_call_target="tpu_custom_call" | custom-call | flops 4831838208 | bytes 18874368 | tf_op jit(solution)/shard_map/pallas_call | solution.py:418
  48.0 0.7 %copy.10 = f32[16,8]{0,1:T(8,128)} copy(f32[16,8]{1,0:T(8,128)S(1)} %get-tuple-element.10) | data formatting | bytes 1024
  48.7 0.7 %copy.13 = bf16[16,8,768]{2,1,0:T(8,128)(2,1)} copy(bf16[16,8,768]{2,1,0:T(8,128)(2,1)S(1)} %bitcast.5) | data formatting | bytes 393216
  49.4 1.7 %copy.14 = bf16[1,384,4096]{2,1,0:T(8,128)(2,1)} copy(bf16[1,384,4096]{2,1,0:T(8,128)(2,1)S(1)} %bitcast.4) | data formatting | bytes 6291456
Async XLA Ops:
  2.1 0.9 %copy-start = (bf16[16,8,768]{2,1,0:T(8,128)(2,1)S(1)}, bf16[16,8,768]{2,1,0:T(8,128)(2,1)}, u32[]{:S(2)}) copy-start(bf16[16,8,768]{2,1,0:T(8,128)(2,1)} %param.6) | copy-start | bytes 589828
  3.1 0.9 %copy-start.1 = (bf16[16,4096]{1,0:T(8,128)(2,1)S(1)}, bf16[16,4096]{1,0:T(8,128)(2,1)}, u32[]{:S(2)}) copy-start(bf16[16,4096]{1,0:T(8,128)(2,1)} %grad_ref.1) | copy-start | bytes 393220

commit v2 on v1

--- a/solution.py
+++ b/solution.py
@@ -117,10 +117,11 @@
 
 
 def gather_kernel(
-    gate_ref, idx_ref, acts_ref, grad_ref, w_hbm,
+    gate_hbm, idx_hbm, acts_hbm, grad_ref, w_hbm,
     act_out, logit_out, down_out,
-    grads, w_buf, acts_send, acts_in, acts_t, hid, back,
-    w_sem, own_sem, g_recv, z_send, x_send, y_send, c_send,
+    gate_ref, idx_ref, acts_ref,
+    grads, w_buf, acts_send, acts_in, acts_t, hid, back, total, down,
+    in_sem, own_sem, out_sem, g_recv, z_send, x_send, y_send, c_send,
     h_send, h_recv, b_send, b_recv,
 ):
     y = lax.axis_index("dp")
@@ -130,7 +131,7 @@
     c = lax.rem(me, CS)
     n_exp = ZS * XS * CS
     n_dev = 2 * n_exp
-    tok, top = idx_ref.shape
+    top, tok = idx_ref.shape
     routed, width = acts_ref.shape
     half = width // 2
     model = grad_ref.shape[1]
@@ -152,24 +153,82 @@
         return carry
 
     lax.fori_loop(1, n_dev, greet, 0)
-    w_copy = pltpu.make_async_copy(w_hbm, w_buf, w_sem)
-    w_copy.start()
     own_grad = pltpu.make_async_copy(grad_ref, grads.at[own], own_sem.at[0])
     own_grad.start()
-
+    loads = [
+        pltpu.make_async_copy(src, dst, in_sem.at[at])
+        for at, (src, dst) in enumerate(
+            ((gate_hbm, gate_ref), (idx_hbm, idx_ref), (acts_hbm, acts_ref), (w_hbm, w_buf))
+        )
+    ]
+    for load in loads:
+        load.start()
+    own_grad.wait()
+    pl.semaphore_wait(barrier, n_dev - 1)
+
+    def grad_copy(src, slot, sem, yy, ee):
+        return pltpu.make_async_remote_copy(
+            src_ref=src, dst_ref=grads.at[slot], send_sem=sem, recv_sem=g_recv.at[slot],
+            device_id=dev(yy, ee), device_id_type=MESH,
+        )
+
+    def arrived(slot):
+        grad_copy(grads.at[slot], slot, c_send.at[0], y, expert_of(x, z, 1 - c)).wait_recv()
+
+    sent = []
+
+    def send(copy, when=None):
+        if when is None:
+            copy.start()
+        else:
+            pl.when(when)(copy.start)
+        sent.append((when, copy))
+
+    def pass_on(src, yy, xx, zz, to_x, to_y, when=None):
+        slot = slot_of(yy, xx, zz, c)
+        in_plane = xx * ZS + zz
+        if to_x:
+            at = zz if yy is y else ZS
+            send(grad_copy(src, slot, x_send.at[at], y, expert_of(1 - x, z, c)), when)
+        if to_y:
+            send(grad_copy(src, slot, y_send.at[in_plane], 1 - y, me), when)
+        send(
+            grad_copy(src, slot, c_send.at[yy * XS * ZS + in_plane], y, expert_of(x, z, 1 - c)),
+            when,
+        )
+
+    def along_z(src, zz, way, when):
+        slot = slot_of(y, x, zz, c)
+        send(
+            grad_copy(
+                src, slot, z_send.at[(way + 1) // 2, zz], y, expert_of(x, z + way, c)
+            ),
+            when,
+        )
+
+    for way in (1, -1):
+        along_z(grads.at[own], z, way, (z + way >= 0) & (z + way < ZS))
+    pass_on(grads.at[own], y, x, z, True, True)
+
+    for load in loads[:3]:
+        load.wait()
     gate = gate_ref[...]
     gate_half = gate.astype(jnp.bfloat16).astype(jnp.float32)
     idx = idx_ref[...].astype(jnp.float32)
     lane = lax.broadcasted_iota(jnp.int32, (tok, routed), 1)
     line = lax.broadcasted_iota(jnp.int32, (tok, routed), 0)
-    gate_wide = jnp.zeros((tok, routed), jnp.float32)
-    idx_wide = jnp.zeros((tok, routed), jnp.float32)
-    for k in range(top):
-        here = (lane == line * top + k)
-        gate_wide = jnp.where(here, gate_half[:, k:k + 1], gate_wide)
-        idx_wide = jnp.where(here, idx[:, k:k + 1], idx_wide)
-    gate_row = jnp.sum(gate_wide, axis=0, keepdims=True)
-    idx_row = jnp.sum(idx_wide, axis=0, keepdims=True)
+    widen = (lax.div(lane, top) == line).astype(jnp.float32)
+    own_row = lax.broadcasted_iota(jnp.int32, (top, routed), 0) == lax.rem(
+        lax.broadcasted_iota(jnp.int32, (top, routed), 1), top
+    )
+    gate_row = jnp.sum(
+        jnp.where(own_row, jnp.dot(gate_half, widen, preferred_element_type=jnp.float32), 0.0),
+        axis=0, keepdims=True,
+    )
+    idx_row = jnp.sum(
+        jnp.where(own_row, jnp.dot(idx, widen, preferred_element_type=jnp.float32), 0.0),
+        axis=0, keepdims=True,
+    )
     rows = n_exp * tok
     row = lax.broadcasted_iota(jnp.int32, (rows, routed), 0)
     col = lax.broadcasted_iota(jnp.int32, (rows, routed), 1)
@@ -182,51 +241,6 @@
     acts_send[0] = weighted[:, :, :half]
     acts_send[1] = weighted[:, :, half:]
 
-    pl.semaphore_wait(barrier, n_dev - 1)
-
-    def grad_copy(src, slot, sem, yy, ee):
-        return pltpu.make_async_remote_copy(
-            src_ref=src, dst_ref=grads.at[slot], send_sem=sem, recv_sem=g_recv.at[slot],
-            device_id=dev(yy, ee), device_id_type=MESH,
-        )
-
-    def arrived(slot):
-        grad_copy(grad_ref, slot, c_send.at[0], y, expert_of(x, z, 1 - c)).wait_recv()
-
-    sent = []
-
-    def send(copy, when=None):
-        if when is None:
-            copy.start()
-        else:
-            pl.when(when)(copy.start)
-        sent.append((when, copy))
-
-    def pass_on(src, yy, xx, zz, to_x, to_y, when=None):
-        slot = slot_of(yy, xx, zz, c)
-        in_plane = xx * ZS + zz
-        if to_x:
-            send(grad_copy(src, slot, x_send.at[zz], y, expert_of(1 - x, z, c)), when)
-        if to_y:
-            send(grad_copy(src, slot, y_send.at[in_plane], 1 - y, me), when)
-        send(
-            grad_copy(src, slot, c_send.at[yy * XS * ZS + in_plane], y, expert_of(x, z, 1 - c)),
-            when,
-        )
-
-    def along_z(src, zz, way, when):
-        slot = slot_of(y, x, zz, c)
-        send(
-            grad_copy(
-                src, slot, z_send.at[(way + 1) // 2, zz], y, expert_of(x, z + way, c)
-            ),
-            when,
-        )
-
-    for way in (1, -1):
-        along_z(grad_ref, z, way, (z + way >= 0) & (z + way < ZS))
-    pass_on(grad_ref, y, x, z, True, True)
-
     def from_z(dist):
         for way in (1, -1):
             zz = z - way * dist
@@ -245,7 +259,7 @@
                 pl.when(there)(functools.partial(arrived, slot))
             else:
                 arrived(slot)
-            pass_on(grads.at[slot], y, 1 - x, zz, False, True, there)
+            pass_on(grads.at[slot], y, 1 - x, zz, False, dist != 2, there)
 
     def acts_copy(r):
         other = lax.rem(lid + r, n_dev)
@@ -294,8 +308,7 @@
     lax.fori_loop(1, n_dev, acts_start, 0)
     own_acts.start()
     from_x(2)
-    own_grad.wait()
-    w_copy.wait()
+    loads[3].wait()
     for zz in range(ZS):
         arrived(slot_of(y, x, zz, 1 - c))
     hidden(x)
@@ -312,46 +325,60 @@
         at = lax.rem(z * CS + c + r, per_x)
         back_copy((1 - x) * per_x + at, lax.div(at, CS), 1 - x, lax.rem(at, CS)).start()
 
-    for xx in (x, 1 - x):
-        for zz in range(ZS):
+    def from_group(xx, dist, to_x):
+        for way in (1, -1) if dist else (1,):
+            zz = z - way * dist
+            there = (zz >= 0) & (zz < ZS) if dist else None
             slot = slot_of(1 - y, xx, zz, c)
-            arrived(slot)
-            pass_on(grads.at[slot], 1 - y, xx, zz, False, False)
-
-    def acts_wait(r, carry):
-        other = lax.rem(lid + r, n_dev)
-        yy, ee = lax.div(other, n_exp), lax.rem(other, n_exp)
+            if dist:
+                pl.when(there)(functools.partial(arrived, slot))
+            else:
+                arrived(slot)
+            pass_on(grads.at[slot], 1 - y, xx, zz, to_x, False, there)
+
+    def acts_wait(r, group):
+        ee = lax.rem(me + r, n_exp)
         slot = slot_of(
-            yy, lax.rem(lax.div(ee, CS), XS), lax.div(ee, XS * CS), lax.rem(ee, CS)
+            group, lax.rem(lax.div(ee, CS), XS), lax.div(ee, XS * CS), lax.rem(ee, CS)
         )
         pltpu.make_async_remote_copy(
             src_ref=acts_send.at[0, 0], dst_ref=acts_in.at[slot],
-            send_sem=h_send.at[r], recv_sem=h_recv.at[slot],
-            device_id=dev(yy, ee), device_id_type=MESH,
+            send_sem=h_send.at[0], recv_sem=h_recv.at[slot],
+            device_id=dev(1 - y, me), device_id_type=MESH,
         ).wait_recv()
-        return carry
-
-    lax.fori_loop(1, n_dev, acts_wait, 0)
+        return group
+
+    def turn(group, at):
+        rows_in = acts_in[pl.ds(group * n_exp, n_exp)].reshape(n_exp * tok, half)
+        acts_t[at] = rows_in.T
+
+    def down_part(group, at, cols):
+        return jnp.dot(
+            acts_t[at], grads[pl.ds(group * n_exp, n_exp), :, cols].reshape(n_exp * tok, tile),
+            preferred_element_type=jnp.float32,
+        )
+
+    for dist in range(ZS):
+        from_group(x, dist, dist == 2)
+
+    lax.fori_loop(1, n_exp, acts_wait, y)
     own_acts.wait()
-    acts_t[...] = acts_in[...].reshape(n_dev * tok, half).T
-    for xx in range(XS):
-        for zz in range(ZS):
-            arrived(slot_of(1 - y, xx, zz, 1 - c))
+    turn(y, 0)
 
     @pl.loop(0, model // tile)
     def _(n):
         cols = pl.ds(pl.multiple_of(n * tile, tile), tile)
-        down_out[:, cols] = jnp.dot(
-            acts_t[...], grads[:, :, cols].reshape(n_dev * tok, tile),
-            preferred_element_type=jnp.float32,
-        ).astype(jnp.bfloat16)
+        total[:, cols] = down_part(y, 0, cols)
+
+    for dist in range(ZS):
+        from_group(1 - x, dist, False)
 
     def back_wait(r, carry):
         ee = lax.rem(me + r, n_exp)
         pltpu.make_async_remote_copy(
             src_ref=hid.at[0], dst_ref=back.at[ee],
             send_sem=b_send.at[0], recv_sem=b_recv.at[ee],
-            device_id=dev(y, ee), device_id_type=MESH,
+            device_id=dev(1 - y, me), device_id_type=MESH,
         ).wait_recv()
         return carry
 
@@ -364,13 +391,15 @@
         lax.broadcasted_iota(jnp.int32, (routed, top), 1)
         == lax.rem(lax.broadcasted_iota(jnp.int32, (routed, top), 0), top)
     ).astype(jnp.float32)
-    gate_col = jnp.sum(
-        jnp.dot(spread, gate_half, preferred_element_type=jnp.float32) * own_k,
-        axis=1, keepdims=True,
-    )
-    idx_col = jnp.sum(
-        jnp.dot(spread, idx, preferred_element_type=jnp.float32) * own_k, axis=1, keepdims=True
-    )
+
+    def column(of):
+        wide = lax.dot_general(
+            spread, of, (((1,), (1,)), ((), ())), preferred_element_type=jnp.float32
+        )
+        return jnp.sum(wide * own_k, axis=1, keepdims=True)
+
+    gate_col = column(gate_half)
+    idx_col = column(idx)
     row = lax.broadcasted_iota(jnp.int32, (routed, rows), 0)
     col = lax.broadcasted_iota(jnp.int32, (routed, rows), 1)
     pick = (
@@ -381,11 +410,24 @@
     act_out[...] = (gate_col * picked).astype(jnp.bfloat16)
     score = jnp.sum(picked * acts_ref[...].astype(jnp.float32), axis=1, keepdims=True)
     score = score.astype(jnp.bfloat16).astype(jnp.float32)
-    gather = (
-        lax.div(lane, top) == line
-    ).astype(jnp.float32)
-    score = jnp.dot(gather, score * own_k, preferred_element_type=jnp.float32)
-    logit_out[...] = gate * (score - jnp.sum(gate * score, axis=1, keepdims=True))
+    score = jnp.dot(own_row.astype(jnp.float32), score * spread, preferred_element_type=jnp.float32)
+    logit_out[...] = gate * (score - jnp.sum(gate * score, axis=0, keepdims=True))
+
+    lax.fori_loop(0, n_exp, acts_wait, 1 - y)
+    turn(1 - y, 1)
+    for xx in (x, 1 - x):
+        for zz in range(ZS):
+            arrived(slot_of(1 - y, xx, zz, 1 - c))
+
+    def down_copy(n):
+        cols = pl.ds(pl.multiple_of(n * tile, tile), tile)
+        return pltpu.make_async_copy(down.at[:, cols], down_out.at[:, cols], out_sem.at[n])
+
+    @pl.loop(0, model // tile)
+    def _(n):
+        cols = pl.ds(pl.multiple_of(n * tile, tile), tile)
+        down[:, cols] = (total[:, cols] + down_part(1 - y, 1, cols)).astype(jnp.bfloat16)
+        down_copy(n).start()
 
     for when, copy in sent:
         if when is None:
@@ -404,6 +446,10 @@
     for r in range(per_x):
         at = lax.rem(z * CS + c + r, per_x)
         back_copy((1 - x) * per_x + at, lax.div(at, CS), 1 - x, lax.rem(at, CS)).wait_send()
+
+    @pl.loop(0, model // tile)
+    def _(n):
+        down_copy(n).wait()
 
 
 def gathered_shards(out_grad, hidden_acts, gate_weights, expert_idx, down_weight):
@@ -415,28 +461,35 @@
     n_dev = 2 * n_exp
     dma = pltpu.SemaphoreType.DMA
     vmem = pl.BlockSpec(memory_space=pltpu.VMEM)
+    hbm = pl.BlockSpec(memory_space=pltpu.HBM)
     act, logit, down = pl.pallas_call(
         gather_kernel,
         out_shape=(
             jax.ShapeDtypeStruct((tok * top, width), jnp.bfloat16),
-            jax.ShapeDtypeStruct((tok, top), jnp.float32),
+            jax.ShapeDtypeStruct((top, tok), jnp.float32),
             jax.ShapeDtypeStruct((half, model), jnp.bfloat16),
         ),
-        in_specs=[vmem] * 4 + [pl.BlockSpec(memory_space=pl.ANY)],
-        out_specs=(vmem, vmem, vmem),
+        in_specs=[hbm] * 5,
+        out_specs=(vmem, vmem, hbm),
         scratch_shapes=[
+            pltpu.VMEM((top, tok), jnp.float32),
+            pltpu.VMEM((top, tok), jnp.int32),
+            pltpu.VMEM((tok * top, width), jnp.bfloat16),
             pltpu.VMEM((n_dev, tok, model), jnp.bfloat16),
             pltpu.VMEM((width, model), jnp.bfloat16),
             pltpu.VMEM((2, n_exp, tok, half), jnp.bfloat16),
             pltpu.VMEM((n_dev, tok, half), jnp.bfloat16),
-            pltpu.VMEM((half, n_dev * tok), jnp.bfloat16),
+            pltpu.VMEM((2, half, n_exp * tok), jnp.bfloat16),
             pltpu.VMEM((n_exp, tok, width), jnp.bfloat16),
             pltpu.VMEM((n_exp, tok, width), jnp.bfloat16),
-            dma,
+            pltpu.VMEM((half, model), jnp.float32),
+            pltpu.VMEM((half, model), jnp.bfloat16),
+            dma((4,)),
             dma((3,)),
+            dma((model // 256,)),
             dma((n_dev,)),
             dma((2, ZS)),
-            dma((ZS,)),
+            dma((ZS + 1,)),
             dma((XS * ZS,)),
             dma((2 * XS * ZS,)),
             dma((n_dev,)),
@@ -445,17 +498,17 @@
             dma((n_exp,)),
         ],
         compiler_params=pltpu.CompilerParams(
-            collective_id=0, has_side_effects=True, vmem_limit_bytes=48 * 1024 * 1024
+            collective_id=0, has_side_effects=True, vmem_limit_bytes=56 * 1024 * 1024
         ),
         cost_estimate=pl.CostEstimate(
             flops=6 * n_exp * tok * model * width, bytes_accessed=3 * width * model * 2,
             transcendentals=0,
         ),
     )(
-        gate_weights, expert_idx, hidden_acts.reshape(tok * top, width), out_grad,
+        gate_weights.T, expert_idx.T, hidden_acts.reshape(tok * top, width), out_grad,
         down_weight.reshape(width, model),
     )
-    return act.reshape(tok, top, width), logit, down[None]
+    return act.reshape(tok, top, width), logit.T, down[None]
 
 
 def solution(mesh):

time: 51.5 us -> 52.6 us (1.021)
  Pallas kernels: 44.1 us -> 44.9 us
    pallas_call x1, Pallas kernels: 44.1 us -> 44.9 us  [gathered_shards(): pl.pallas_call(gather_kernel, out_shape=(jax.ShapeDtypeStruct((tok * top,...]
    unnamed x9 -> x3, local copies, waits for them, and re-layouts: 6.35 us -> 6.79 us
where the time goes in v2:
time: 52.6 us; the launch traced here: 52.4 us
  Pallas kernels  44.9 us (85%)
  local copies, waits for them, and re-layouts  6.79 us (13%)
  between operations  0.64 us (1%)
    pallas_call x1, Pallas kernels, gathered_shards(): pl.pallas_call(gather_kernel, out_shape=(jax.ShapeDtypeStruct((tok * top,...  44.9 us
    unnamed x3, local copies, waits for them, and re-layouts  6.79 us

profile of v2, /device:TPU:0, one launch (start us, length us, event | category | flops | bytes accessed | tf_op | source)
XLA Modules:
  0.0 52.4 jit_solution(6733399255930715970)
XLA Ops:
  0.6 44.9 %shard_map.76 = (bf16[128,768]{1,0:T(8,128)(2,1)}, f32[8,16]{1,0:T(8,128)}, bf16[384,4096]{1,0:T(8,128)(2,1)}) custom-call(f32[8,16]{1,0:T(8,128)} %bitcast.12, s32[8,16]{1,0:T(8,128)} %bitcast.13, bf16[128,768]{1,0:T(8,128)(2,1)} %bitcast.11, bf16[16,4096]{1,0:T(8,128)(2,1)} %grad_ref.1, bf16[768,4096]{1,0:T(8,128)(2,1)} %bitcast.10), custom_call_target="tpu_custom_call" | custom-call | flops 4831838208 | bytes 18874368 | tf_op jit(solution)/shard_map/pallas_call | solution.py:465
  45.6 1.6 %copy.11 = bf16[16,8,768]{2,1,0:T(8,128)(2,1)} copy(bf16[16,8,768]{2,1,0:T(8,128)(2,1)} %bitcast.8) | data formatting | bytes 393216
  47.2 1.3 %copy.12 = f32[16,8]{0,1:T(8,128)} copy(f32[16,8]{0,1:T(8,128)} %bitcast.9) | data formatting | bytes 1024
  48.4 3.9 %copy.13 = bf16[1,384,4096]{2,1,0:T(8,128)(2,1)} copy(bf16[1,384,4096]{2,1,0:T(8,128)(2,1)} %bitcast.7) | data formatting | bytes 6291456

commit v3 on v2

--- a/solution.py
+++ b/solution.py
@@ -120,8 +120,8 @@
     gate_hbm, idx_hbm, acts_hbm, grad_ref, w_hbm,
     act_out, logit_out, down_out,
     gate_ref, idx_ref, acts_ref,
-    grads, w_buf, acts_send, acts_in, acts_t, hid, back, total, down,
-    in_sem, own_sem, out_sem, g_recv, z_send, x_send, y_send, c_send,
+    grads, w_buf, acts_send, acts_in, acts_t, hid, back, total,
+    in_sem, own_sem, g_recv, z_send, x_send, y_send, c_send,
     h_send, h_recv, b_send, b_recv,
 ):
     y = lax.axis_index("dp")
@@ -241,6 +241,29 @@
     acts_send[0] = weighted[:, :, :half]
     acts_send[1] = weighted[:, :, half:]
 
+    tall_row = lax.broadcasted_iota(jnp.int32, (routed, tok), 0)
+    tall_col = lax.broadcasted_iota(jnp.int32, (routed, tok), 1)
+    spread = (lax.div(tall_row, top) == tall_col).astype(jnp.float32)
+    own_k = (
+        lax.broadcasted_iota(jnp.int32, (routed, top), 1)
+        == lax.rem(lax.broadcasted_iota(jnp.int32, (routed, top), 0), top)
+    ).astype(jnp.float32)
+
+    def column(of):
+        wide = lax.dot_general(
+            spread, of, (((1,), (1,)), ((), ())), preferred_element_type=jnp.float32
+        )
+        return jnp.sum(wide * own_k, axis=1, keepdims=True)
+
+    gate_col = column(gate_half)
+    idx_col = column(idx)
+    row = lax.broadcasted_iota(jnp.int32, (routed, rows), 0)
+    col = lax.broadcasted_iota(jnp.int32, (routed, rows), 1)
+    pick = (
+        (idx_col == lax.div(col, tok).astype(jnp.float32))
+        & (lax.div(row, top) == lax.rem(col, tok))
+    ).astype(jnp.float32).astype(jnp.bfloat16)
+
     def from_z(dist):
         for way in (1, -1):
             zz = z - way * dist
@@ -284,46 +307,14 @@
         )
 
     per_x = ZS * CS
-    tile = 256
-
-    def hidden(xx):
-        lhs = grads[pl.ds(slot_of(y, xx, 0, 0), per_x)].reshape(per_x * tok, model)
-
-        @pl.loop(0, width // tile)
-        def _(n):
-            cols = pl.ds(pl.multiple_of(n * tile, tile), tile)
-            part = lax.dot_general(
-                lhs, w_buf[cols, :], (((1,), (1,)), ((), ())),
-                preferred_element_type=jnp.float32,
-            )
-            hid[pl.ds(xx * per_x, per_x), :, cols] = part.astype(jnp.bfloat16).reshape(
-                per_x, tok, tile
-            )
-
-    from_z(1)
-    from_x(0)
-    from_z(2)
-    from_x(1)
-    from_z(3)
-    lax.fori_loop(1, n_dev, acts_start, 0)
-    own_acts.start()
-    from_x(2)
-    loads[3].wait()
-    for zz in range(ZS):
-        arrived(slot_of(y, x, zz, 1 - c))
-    hidden(x)
-    own_back = pltpu.make_async_copy(hid.at[own - y * n_exp], back.at[me], own_sem.at[2])
-    own_back.start()
-    for r in range(1, per_x):
-        at = lax.rem(z * CS + c + r, per_x)
-        back_copy(x * per_x + at, lax.div(at, CS), x, lax.rem(at, CS)).start()
-    from_x(3)
-    for zz in range(ZS):
-        arrived(slot_of(y, 1 - x, zz, 1 - c))
-    hidden(1 - x)
-    for r in range(per_x):
-        at = lax.rem(z * CS + c + r, per_x)
-        back_copy((1 - x) * per_x + at, lax.div(at, CS), 1 - x, lax.rem(at, CS)).start()
+    tile = model // 4
+
+    def hidden():
+        part = lax.dot_general(
+            grads[pl.ds(y * n_exp, n_exp)].reshape(n_exp * tok, model), w_buf[...],
+            (((1,), (1,)), ((), ())), preferred_element_type=jnp.float32,
+        )
+        hid[...] = part.astype(jnp.bfloat16).reshape(n_exp, tok, width)
 
     def from_group(xx, dist, to_x):
         for way in (1, -1) if dist else (1,):
@@ -336,6 +327,35 @@
                 arrived(slot)
             pass_on(grads.at[slot], 1 - y, xx, zz, to_x, False, there)
 
+    from_z(1)
+    from_x(0)
+    from_z(2)
+    from_x(1)
+    from_z(3)
+    lax.fori_loop(1, n_dev, acts_start, 0)
+    own_acts.start()
+    from_x(2)
+    from_x(3)
+    for dist in range(2):
+        from_group(x, dist, False)
+    loads[3].wait()
+    for xx in (x, 1 - x):
+        for zz in range(ZS):
+            arrived(slot_of(y, xx, zz, 1 - c))
+    hidden()
+    own_back = pltpu.make_async_copy(hid.at[own - y * n_exp], back.at[me], own_sem.at[2])
+    own_back.start()
+
+    def each_back():
+        for xx in (1 - x, x):
+            for r in range(per_x):
+                at = lax.rem(z * CS + c + r, per_x)
+                if xx is not x or r:
+                    yield back_copy(xx * per_x + at, lax.div(at, CS), xx, lax.rem(at, CS))
+
+    for copy in each_back():
+        copy.start()
+
     def acts_wait(r, group):
         ee = lax.rem(me + r, n_exp)
         slot = slot_of(
@@ -358,7 +378,7 @@
             preferred_element_type=jnp.float32,
         )
 
-    for dist in range(ZS):
+    for dist in range(2, ZS):
         from_group(x, dist, dist == 2)
 
     lax.fori_loop(1, n_exp, acts_wait, y)
@@ -384,28 +404,6 @@
 
     lax.fori_loop(1, n_exp, back_wait, 0)
     own_back.wait()
-    tall_row = lax.broadcasted_iota(jnp.int32, (routed, tok), 0)
-    tall_col = lax.broadcasted_iota(jnp.int32, (routed, tok), 1)
-    spread = (lax.div(tall_row, top) == tall_col).astype(jnp.float32)
-    own_k = (
-        lax.broadcasted_iota(jnp.int32, (routed, top), 1)
-        == lax.rem(lax.broadcasted_iota(jnp.int32, (routed, top), 0), top)
-    ).astype(jnp.float32)
-
-    def column(of):
-        wide = lax.dot_general(
-            spread, of, (((1,), (1,)), ((), ())), preferred_element_type=jnp.float32
-        )
-        return jnp.sum(wide * own_k, axis=1, keepdims=True)
-
-    gate_col = column(gate_half)
-    idx_col = column(idx)
-    row = lax.broadcasted_iota(jnp.int32, (routed, rows), 0)
-    col = lax.broadcasted_iota(jnp.int32, (routed, rows), 1)
-    pick = (
-        (idx_col == lax.div(col, tok).astype(jnp.float32))
-        & (lax.div(row, top) == lax.rem(col, tok))
-    ).astype(jnp.float32).astype(jnp.bfloat16)
     picked = jnp.dot(pick, back[...].reshape(rows, width), preferred_element_type=jnp.float32)
     act_out[...] = (gate_col * picked).astype(jnp.bfloat16)
     score = jnp.sum(picked * acts_ref[...].astype(jnp.float32), axis=1, keepdims=True)
@@ -419,15 +417,10 @@
         for zz in range(ZS):
             arrived(slot_of(1 - y, xx, zz, 1 - c))
 
-    def down_copy(n):
-        cols = pl.ds(pl.multiple_of(n * tile, tile), tile)
-        return pltpu.make_async_copy(down.at[:, cols], down_out.at[:, cols], out_sem.at[n])
-
     @pl.loop(0, model // tile)
     def _(n):
         cols = pl.ds(pl.multiple_of(n * tile, tile), tile)
-        down[:, cols] = (total[:, cols] + down_part(1 - y, 1, cols)).astype(jnp.bfloat16)
-        down_copy(n).start()
+        down_out[:, cols] = (total[:, cols] + down_part(1 - y, 1, cols)).astype(jnp.bfloat16)
 
     for when, copy in sent:
         if when is None:
@@ -440,16 +433,8 @@
         return carry
 
     lax.fori_loop(1, n_dev, acts_sent, 0)
-    for r in range(1, per_x):
-        at = lax.rem(z * CS + c + r, per_x)
-        back_copy(x * per_x + at, lax.div(at, CS), x, lax.rem(at, CS)).wait_send()
-    for r in range(per_x):
-        at = lax.rem(z * CS + c + r, per_x)
-        back_copy((1 - x) * per_x + at, lax.div(at, CS), 1 - x, lax.rem(at, CS)).wait_send()
-
-    @pl.loop(0, model // tile)
-    def _(n):
-        down_copy(n).wait()
+    for copy in each_back():
+        copy.wait_send()
 
 
 def gathered_shards(out_grad, hidden_acts, gate_weights, expert_idx, down_weight):
@@ -470,7 +455,7 @@
             jax.ShapeDtypeStruct((half, model), jnp.bfloat16),
         ),
         in_specs=[hbm] * 5,
-        out_specs=(vmem, vmem, hbm),
+        out_specs=(vmem, vmem, vmem),
         scratch_shapes=[
             pltpu.VMEM((top, tok), jnp.float32),
             pltpu.VMEM((top, tok), jnp.int32),
@@ -483,10 +468,8 @@
             pltpu.VMEM((n_exp, tok, width), jnp.bfloat16),
             pltpu.VMEM((n_exp, tok, width), jnp.bfloat16),
             pltpu.VMEM((half, model), jnp.float32),
-            pltpu.VMEM((half, model), jnp.bfloat16),
             dma((4,)),
             dma((3,)),
-            dma((model // 256,)),
             dma((n_dev,)),
             dma((2, ZS)),
             dma((ZS + 1,)),
@@ -498,15 +481,20 @@
             dma((n_exp,)),
         ],
         compiler_params=pltpu.CompilerParams(
-            collective_id=0, has_side_effects=True, vmem_limit_bytes=56 * 1024 * 1024
+            collective_id=0, has_side_effects=True, vmem_limit_bytes=36 * 1024 * 1024
         ),
         cost_estimate=pl.CostEstimate(
             flops=6 * n_exp * tok * model * width, bytes_accessed=3 * width * model * 2,
             transcendentals=0,
         ),
     )(
-        gate_weights.T, expert_idx.T, hidden_acts.reshape(tok * top, width), out_grad,
-        down_weight.reshape(width, model),
+        *(
+            pltpu.with_memory_space_constraint(array, pltpu.HBM)
+            for array in (
+                gate_weights.T, expert_idx.T, hidden_acts.reshape(tok * top, width), out_grad,
+                down_weight.reshape(width, model),
+            )
+        )
     )
     return act.reshape(tok, top, width), logit.T, down[None]
 

time: 52.6 us -> 43.8 us (0.83)
  Pallas kernels: 44.9 us -> 40.1 us
  local copies, waits for them, and re-layouts: 6.79 us -> 2.94 us
    pallas_call x1, Pallas kernels: 44.9 us -> 40.1 us  [gathered_shards(): pl.pallas_call(gather_kernel, out_shape=(jax.ShapeDtypeStruct((tok * top,...]
    unnamed x3, local copies, waits for them, and re-layouts: 6.79 us -> 2.94 us
where the time goes in v3:
time: 43.8 us; the launch traced here: 43.6 us
  Pallas kernels  40.1 us (92%)
  local copies, waits for them, and re-layouts  2.94 us (7%)
  between operations  0.64 us (1%)
    pallas_call x1, Pallas kernels, gathered_shards(): pl.pallas_call(gather_kernel, out_shape=(jax.ShapeDtypeStruct((tok * top,...  40.1 us
    unnamed x3, local copies, waits for them, and re-layouts  2.94 us

profile of v3, /device:TPU:0, one launch (start us, length us, event | category | flops | bytes accessed | tf_op | source)
XLA Modules:
  0.0 43.6 jit_solution(8607629004942858904)
XLA Ops:
  0.6 40.1 %shard_map.76 = (bf16[128,768]{1,0:T(8,128)(2,1)S(1)}, f32[8,16]{1,0:T(8,128)S(1)}, bf16[384,4096]{1,0:T(8,128)(2,1)S(1)}) custom-call(f32[8,16]{1,0:T(8,128)} %bitcast.12, s32[8,16]{1,0:T(8,128)} %bitcast.13, bf16[128,768]{1,0:T(8,128)(2,1)} %bitcast.11, bf16[16,4096]{1,0:T(8,128)(2,1)} %grad_ref.1, bf16[768,4096]{1,0:T(8,128)(2,1)} %bitcast.10), custom_call_target="tpu_custom_call" | custom-call | flops 4831838208 | bytes 18874368 | tf_op jit(solution)/shard_map/pallas_call | solution.py:450
  40.7 0.7 %copy.11 = bf16[16,8,768]{2,1,0:T(8,128)(2,1)} copy(bf16[16,8,768]{2,1,0:T(8,128)(2,1)S(1)} %bitcast.8) | data formatting | bytes 393216
  41.4 0.6 %copy.12 = f32[16,8]{0,1:T(8,128)} copy(f32[16,8]{0,1:T(8,128)S(1)} %bitcast.9) | data formatting | bytes 1024
  42.0 1.7 %copy.13 = bf16[1,384,4096]{2,1,0:T(8,128)(2,1)} copy(bf16[1,384,4096]{2,1,0:T(8,128)(2,1)S(1)} %bitcast.7) | data formatting | bytes 6291456

commit v4 on v3

--- a/solution.py
+++ b/solution.py
@@ -9,6 +9,7 @@
 
 MESH = pl.DeviceIdType.MESH
 ZS, XS, CS = 4, 2, 2
+PARTS = 2
 
 
 def routed_shards(out_grad, hidden_acts, gate_weights, expert_idx, down_weight):
@@ -120,7 +121,7 @@
     gate_hbm, idx_hbm, acts_hbm, grad_ref, w_hbm,
     act_out, logit_out, down_out,
     gate_ref, idx_ref, acts_ref,
-    grads, w_buf, acts_send, acts_in, acts_t, hid, back, total,
+    grads, w_buf, acts_send, acts_in, acts_t, hid, hid_sum, back, total,
     in_sem, own_sem, g_recv, z_send, x_send, y_send, c_send,
     h_send, h_recv, b_send, b_recv,
 ):
@@ -153,8 +154,15 @@
         return carry
 
     lax.fori_loop(1, n_dev, greet, 0)
-    own_grad = pltpu.make_async_copy(grad_ref, grads.at[own], own_sem.at[0])
-    own_grad.start()
+    part_cols = model // PARTS
+    own_grads = [
+        pltpu.make_async_copy(
+            grad_ref.at[:, pl.ds(p * part_cols, part_cols)], grads.at[p, own], own_sem.at[2 + p]
+        )
+        for p in range(PARTS)
+    ]
+    for copy in own_grads:
+        copy.start()
     loads = [
         pltpu.make_async_copy(src, dst, in_sem.at[at])
         for at, (src, dst) in enumerate(
@@ -163,17 +171,19 @@
     ]
     for load in loads:
         load.start()
-    own_grad.wait()
+    for copy in own_grads:
+        copy.wait()
     pl.semaphore_wait(barrier, n_dev - 1)
 
-    def grad_copy(src, slot, sem, yy, ee):
+    def grad_copy(p, slot, sem, yy, ee):
+        block = grads.at[p, slot]
         return pltpu.make_async_remote_copy(
-            src_ref=src, dst_ref=grads.at[slot], send_sem=sem, recv_sem=g_recv.at[slot],
+            src_ref=block, dst_ref=block, send_sem=sem, recv_sem=g_recv.at[p, slot],
             device_id=dev(yy, ee), device_id_type=MESH,
         )
 
-    def arrived(slot):
-        grad_copy(grads.at[slot], slot, c_send.at[0], y, expert_of(x, z, 1 - c)).wait_recv()
+    def arrived(p, slot):
+        grad_copy(p, slot, c_send.at[p, 0], y, expert_of(x, z, 1 - c)).wait_recv()
 
     sent = []
 
@@ -184,31 +194,26 @@
             pl.when(when)(copy.start)
         sent.append((when, copy))
 
-    def pass_on(src, yy, xx, zz, to_x, to_y, when=None):
+    def pass_on(p, yy, xx, zz, to_x, to_y, when=None):
         slot = slot_of(yy, xx, zz, c)
         in_plane = xx * ZS + zz
         if to_x:
             at = zz if yy is y else ZS
-            send(grad_copy(src, slot, x_send.at[at], y, expert_of(1 - x, z, c)), when)
+            send(grad_copy(p, slot, x_send.at[p, at], y, expert_of(1 - x, z, c)), when)
         if to_y:
-            send(grad_copy(src, slot, y_send.at[in_plane], 1 - y, me), when)
-        send(
-            grad_copy(src, slot, c_send.at[yy * XS * ZS + in_plane], y, expert_of(x, z, 1 - c)),
-            when,
-        )
-
-    def along_z(src, zz, way, when):
+            send(grad_copy(p, slot, y_send.at[p, in_plane], 1 - y, me), when)
+        at = yy * XS * ZS + in_plane
+        send(grad_copy(p, slot, c_send.at[p, at], y, expert_of(x, z, 1 - c)), when)
+
+    def along_z(p, zz, way, when):
         slot = slot_of(y, x, zz, c)
-        send(
-            grad_copy(
-                src, slot, z_send.at[(way + 1) // 2, zz], y, expert_of(x, z + way, c)
-            ),
-            when,
-        )
-
-    for way in (1, -1):
-        along_z(grads.at[own], z, way, (z + way >= 0) & (z + way < ZS))
-    pass_on(grads.at[own], y, x, z, True, True)
+        sem = z_send.at[p, (way + 1) // 2, zz]
+        send(grad_copy(p, slot, sem, y, expert_of(x, z + way, c)), when)
+
+    for p in range(PARTS):
+        for way in (1, -1):
+            along_z(p, z, way, (z + way >= 0) & (z + way < ZS))
+        pass_on(p, y, x, z, True, True)
 
     for load in loads[:3]:
         load.wait()
@@ -264,25 +269,27 @@
         & (lax.div(row, top) == lax.rem(col, tok))
     ).astype(jnp.float32).astype(jnp.bfloat16)
 
-    def from_z(dist):
-        for way in (1, -1):
-            zz = z - way * dist
-            there = (zz >= 0) & (zz < ZS)
-            slot = slot_of(y, x, zz, c)
-            pl.when(there)(functools.partial(arrived, slot))
-            along_z(grads.at[slot], zz, way, there & (z + way >= 0) & (z + way < ZS))
-            pass_on(grads.at[slot], y, x, zz, True, True, there)
-
-    def from_x(dist):
+    def receive(p, yy, xx, dist, to_z, to_x, to_y):
         for way in (1, -1) if dist else (1,):
             zz = z - way * dist
             there = (zz >= 0) & (zz < ZS) if dist else None
-            slot = slot_of(y, 1 - x, zz, c)
+            slot = slot_of(yy, xx, zz, c)
             if dist:
-                pl.when(there)(functools.partial(arrived, slot))
+                pl.when(there)(functools.partial(arrived, p, slot))
             else:
-                arrived(slot)
-            pass_on(grads.at[slot], y, 1 - x, zz, False, dist != 2, there)
+                arrived(p, slot)
+            if to_z:
+                along_z(p, zz, way, there & (z + way >= 0) & (z + way < ZS))
+            pass_on(p, yy, xx, zz, to_x, to_y, there)
+
+    def from_z(p, dist):
+        receive(p, y, x, dist, True, True, True)
+
+    def from_x(p, dist):
+        receive(p, y, 1 - x, dist, False, False, dist != 2)
+
+    def from_group(p, xx, dist):
+        receive(p, 1 - y, xx, dist, False, xx is x and dist == 2, False)
 
     def acts_copy(r):
         other = lax.rem(lid + r, n_dev)
@@ -309,41 +316,48 @@
     per_x = ZS * CS
     tile = model // 4
 
-    def hidden():
+    def hidden(p):
         part = lax.dot_general(
-            grads[pl.ds(y * n_exp, n_exp)].reshape(n_exp * tok, model), w_buf[...],
+            grads[p, pl.ds(y * n_exp, n_exp)].reshape(n_exp * tok, part_cols),
+            w_buf[:, pl.ds(p * part_cols, part_cols)],
             (((1,), (1,)), ((), ())), preferred_element_type=jnp.float32,
         )
-        hid[...] = part.astype(jnp.bfloat16).reshape(n_exp, tok, width)
-
-    def from_group(xx, dist, to_x):
-        for way in (1, -1) if dist else (1,):
-            zz = z - way * dist
-            there = (zz >= 0) & (zz < ZS) if dist else None
-            slot = slot_of(1 - y, xx, zz, c)
-            if dist:
-                pl.when(there)(functools.partial(arrived, slot))
-            else:
-                arrived(slot)
-            pass_on(grads.at[slot], 1 - y, xx, zz, to_x, False, there)
-
-    from_z(1)
-    from_x(0)
-    from_z(2)
-    from_x(1)
-    from_z(3)
+        if p:
+            part = part + hid_sum[...]
+        if p < PARTS - 1:
+            hid_sum[...] = part
+        else:
+            hid[...] = part.astype(jnp.bfloat16).reshape(n_exp, tok, width)
+
+    def mates(p, group):
+        for xx in (x, 1 - x):
+            for zz in range(ZS):
+                arrived(p, slot_of(group, xx, zz, 1 - c))
+
+    parts = range(PARTS)
+    for p in parts:
+        from_z(p, 1)
+    for p in parts:
+        from_x(p, 0)
+    for p in parts:
+        from_z(p, 2)
+    for p in parts:
+        from_x(p, 1)
+    for p in parts:
+        from_z(p, 3)
     lax.fori_loop(1, n_dev, acts_start, 0)
     own_acts.start()
-    from_x(2)
-    from_x(3)
+    for p in parts:
+        from_x(p, 2)
     for dist in range(2):
-        from_group(x, dist, False)
+        for p in parts:
+            from_group(p, x, dist)
     loads[3].wait()
-    for xx in (x, 1 - x):
-        for zz in range(ZS):
-            arrived(slot_of(y, xx, zz, 1 - c))
-    hidden()
-    own_back = pltpu.make_async_copy(hid.at[own - y * n_exp], back.at[me], own_sem.at[2])
+    for p in parts:
+        from_x(p, 3)
+        mates(p, y)
+        hidden(p)
+    own_back = pltpu.make_async_copy(hid.at[own - y * n_exp], back.at[me], own_sem.at[0])
     own_back.start()
 
     def each_back():
@@ -372,14 +386,17 @@
         rows_in = acts_in[pl.ds(group * n_exp, n_exp)].reshape(n_exp * tok, half)
         acts_t[at] = rows_in.T
 
-    def down_part(group, at, cols):
+    def down_part(group, at, n):
+        p = lax.div(n * tile, part_cols)
+        cols = pl.ds(pl.multiple_of(lax.rem(n * tile, part_cols), tile), tile)
         return jnp.dot(
-            acts_t[at], grads[pl.ds(group * n_exp, n_exp), :, cols].reshape(n_exp * tok, tile),
+            acts_t[at], grads[p, pl.ds(group * n_exp, n_exp), :, cols].reshape(n_exp * tok, tile),
             preferred_element_type=jnp.float32,
         )
 
     for dist in range(2, ZS):
-        from_group(x, dist, dist == 2)
+        for p in parts:
+            from_group(p, x, dist)
 
     lax.fori_loop(1, n_exp, acts_wait, y)
     own_acts.wait()
@@ -388,10 +405,21 @@
     @pl.loop(0, model // tile)
     def _(n):
         cols = pl.ds(pl.multiple_of(n * tile, tile), tile)
-        total[:, cols] = down_part(y, 0, cols)
+        total[:, cols] = down_part(y, 0, n)
 
     for dist in range(ZS):
-        from_group(1 - x, dist, False)
+        for p in parts:
+            from_group(p, 1 - x, dist)
+
+    lax.fori_loop(0, n_exp, acts_wait, 1 - y)
+    turn(1 - y, 1)
+    for p in parts:
+        mates(p, 1 - y)
+
+    @pl.loop(0, model // tile)
+    def _(n):
+        cols = pl.ds(pl.multiple_of(n * tile, tile), tile)
+        down_out[:, cols] = (total[:, cols] + down_part(1 - y, 1, n)).astype(jnp.bfloat16)
 
     def back_wait(r, carry):
         ee = lax.rem(me + r, n_exp)
@@ -410,17 +438,6 @@
     score = score.astype(jnp.bfloat16).astype(jnp.float32)
     score = jnp.dot(own_row.astype(jnp.float32), score * spread, preferred_element_type=jnp.float32)
     logit_out[...] = gate * (score - jnp.sum(gate * score, axis=0, keepdims=True))
-
-    lax.fori_loop(0, n_exp, acts_wait, 1 - y)
-    turn(1 - y, 1)
-    for xx in (x, 1 - x):
-        for zz in range(ZS):
-            arrived(slot_of(1 - y, xx, zz, 1 - c))
-
-    @pl.loop(0, model // tile)
-    def _(n):
-        cols = pl.ds(pl.multiple_of(n * tile, tile), tile)
-        down_out[:, cols] = (total[:, cols] + down_part(1 - y, 1, cols)).astype(jnp.bfloat16)
 
     for when, copy in sent:
         if when is None:
@@ -460,21 +477,22 @@
             pltpu.VMEM((top, tok), jnp.float32),
             pltpu.VMEM((top, tok), jnp.int32),
             pltpu.VMEM((tok * top, width), jnp.bfloat16),
-            pltpu.VMEM((n_dev, tok, model), jnp.bfloat16),
+            pltpu.VMEM((PARTS, n_dev, tok, model // PARTS), jnp.bfloat16),
             pltpu.VMEM((width, model), jnp.bfloat16),
             pltpu.VMEM((2, n_exp, tok, half), jnp.bfloat16),
             pltpu.VMEM((n_dev, tok, half), jnp.bfloat16),
             pltpu.VMEM((2, half, n_exp * tok), jnp.bfloat16),
             pltpu.VMEM((n_exp, tok, width), jnp.bfloat16),
+            pltpu.VMEM((n_exp * tok, width), jnp.float32),
             pltpu.VMEM((n_exp, tok, width), jnp.bfloat16),
             pltpu.VMEM((half, model), jnp.float32),
             dma((4,)),
-            dma((3,)),
-            dma((n_dev,)),
-            dma((2, ZS)),
-            dma((ZS + 1,)),
-            dma((XS * ZS,)),
-            dma((2 * XS * ZS,)),
+            dma((2 + PARTS,)),
+            dma((PARTS, n_dev)),
+            dma((PARTS, 2, ZS)),
+            dma((PARTS, ZS + 1)),
+            dma((PARTS, XS * ZS)),
+            dma((PARTS, 2 * XS * ZS)),
             dma((n_dev,)),
             dma((n_dev,)),
             dma((n_exp,)),

time: 43.8 us -> 43.6 us (level); the launches traced: 43.6 us -> 42.8 us
  Pallas kernels: 40.1 us -> 39.2 us
    pallas_call x1, Pallas kernels: 40.1 us -> 39.2 us  [gathered_shards(): pl.pallas_call(gather_kernel, out_shape=(jax.ShapeDtypeStruct((tok * top,...]
where the time goes in v4:
time: 43.6 us; the launch traced here: 42.8 us
  Pallas kernels  39.2 us (90%)
  local copies, waits for them, and re-layouts  2.94 us (7%)
  between operations  0.64 us (1%)
    pallas_call x1, Pallas kernels, gathered_shards(): pl.pallas_call(gather_kernel, out_shape=(jax.ShapeDtypeStruct((tok * top,...  39.2 us
    unnamed x3, local copies, waits for them, and re-layouts  2.94 us

profile of v4, /device:TPU:0, one launch (start us, length us, event | category | flops | bytes accessed | tf_op | source)
XLA Modules:
  0.0 42.8 jit_solution(15315723217713447789)
XLA Ops:
  0.6 39.2 %shard_map.76 = (bf16[128,768]{1,0:T(8,128)(2,1)S(1)}, f32[8,16]{1,0:T(8,128)S(1)}, bf16[384,4096]{1,0:T(8,128)(2,1)S(1)}) custom-call(f32[8,16]{1,0:T(8,128)} %bitcast.12, s32[8,16]{1,0:T(8,128)} %bitcast.13, bf16[128,768]{1,0:T(8,128)(2,1)} %bitcast.11, bf16[16,4096]{1,0:T(8,128)(2,1)} %grad_ref.1, bf16[768,4096]{1,0:T(8,128)(2,1)} %bitcast.10), custom_call_target="tpu_custom_call" | custom-call | flops 4831838208 | bytes 18874368 | tf_op jit(solution)/shard_map/pallas_call | solution.py:467
  39.8 0.7 %copy.11 = bf16[16,8,768]{2,1,0:T(8,128)(2,1)} copy(bf16[16,8,768]{2,1,0:T(8,128)(2,1)S(1)} %bitcast.8) | data formatting | bytes 393216
  40.5 0.6 %copy.12 = f32[16,8]{0,1:T(8,128)} copy(f32[16,8]{0,1:T(8,128)S(1)} %bitcast.9) | data formatting | bytes 1024
  41.1 1.7 %copy.13 = bf16[1,384,4096]{2,1,0:T(8,128)(2,1)} copy(bf16[1,384,4096]{2,1,0:T(8,128)(2,1)S(1)} %bitcast.7) | data formatting | bytes 6291456

commit v5 on v4

--- a/solution.py
+++ b/solution.py
@@ -9,6 +9,7 @@
 
 MESH = pl.DeviceIdType.MESH
 ZS, XS, CS = 4, 2, 2
+STRIPS = 4
 PARTS = 2
 
 
@@ -142,6 +143,16 @@
     def dev(yy, ee):
         return {"dp": yy, "expert": ee}
 
+    part_cols = model // PARTS
+    own_grads = [
+        pltpu.make_async_copy(
+            grad_ref.at[:, pl.ds(p * part_cols, part_cols)], grads.at[p, own], own_sem.at[2 + p]
+        )
+        for p in range(PARTS)
+    ]
+    for copy in own_grads:
+        copy.start()
+
     barrier = pltpu.get_barrier_semaphore()
 
     def greet(r, carry):
@@ -154,15 +165,6 @@
         return carry
 
     lax.fori_loop(1, n_dev, greet, 0)
-    part_cols = model // PARTS
-    own_grads = [
-        pltpu.make_async_copy(
-            grad_ref.at[:, pl.ds(p * part_cols, part_cols)], grads.at[p, own], own_sem.at[2 + p]
-        )
-        for p in range(PARTS)
-    ]
-    for copy in own_grads:
-        copy.start()
     loads = [
         pltpu.make_async_copy(src, dst, in_sem.at[at])
         for at, (src, dst) in enumerate(
@@ -345,10 +347,10 @@
         from_x(p, 1)
     for p in parts:
         from_z(p, 3)
+    for p in parts:
+        from_x(p, 2)
     lax.fori_loop(1, n_dev, acts_start, 0)
     own_acts.start()
-    for p in parts:
-        from_x(p, 2)
     for dist in range(2):
         for p in parts:
             from_group(p, x, dist)
@@ -398,6 +400,10 @@
         for p in parts:
             from_group(p, x, dist)
 
+    for dist in range(ZS):
+        for p in parts:
+            from_group(p, 1 - x, dist)
+
     lax.fori_loop(1, n_exp, acts_wait, y)
     own_acts.wait()
     turn(y, 0)
@@ -407,10 +413,6 @@
         cols = pl.ds(pl.multiple_of(n * tile, tile), tile)
         total[:, cols] = down_part(y, 0, n)
 
-    for dist in range(ZS):
-        for p in parts:
-            from_group(p, 1 - x, dist)
-
     lax.fori_loop(0, n_exp, acts_wait, 1 - y)
     turn(1 - y, 1)
     for p in parts:
@@ -420,6 +422,20 @@
     def _(n):
         cols = pl.ds(pl.multiple_of(n * tile, tile), tile)
         down_out[:, cols] = (total[:, cols] + down_part(1 - y, 1, n)).astype(jnp.bfloat16)
+
+    for when, copy in sent:
+        if when is None:
+            copy.wait_send()
+        else:
+            pl.when(when)(copy.wait_send)
+
+    def acts_sent(r, carry):
+        acts_copy(r).wait_send()
+        return carry
+
+    lax.fori_loop(1, n_dev, acts_sent, 0)
+    for copy in each_back():
+        copy.wait_send()
 
     def back_wait(r, carry):
         ee = lax.rem(me + r, n_exp)
@@ -439,19 +455,22 @@
     score = jnp.dot(own_row.astype(jnp.float32), score * spread, preferred_element_type=jnp.float32)
     logit_out[...] = gate * (score - jnp.sum(gate * score, axis=0, keepdims=True))
 
-    for when, copy in sent:
-        if when is None:
-            copy.wait_send()
-        else:
-            pl.when(when)(copy.wait_send)
-
-    def acts_sent(r, carry):
-        acts_copy(r).wait_send()
-        return carry
-
-    lax.fori_loop(1, n_dev, acts_sent, 0)
-    for copy in each_back():
-        copy.wait_send()
+
+def store_kernel(*refs):
+    results, outs, sems = refs[:3], refs[3:6], refs[6]
+    copies = []
+    for src, dst in zip(results, outs):
+        rows = src.shape[0]
+        step = rows // STRIPS if rows % (16 * STRIPS) == 0 else rows
+        for at in range(0, rows, step):
+            strip = pl.ds(at, step)
+            copies.append(
+                pltpu.make_async_copy(src.at[strip], dst.at[strip], sems.at[len(copies)])
+            )
+    for copy in copies[::-1]:
+        copy.start()
+    for copy in copies:
+        copy.wait()
 
 
 def gathered_shards(out_grad, hidden_acts, gate_weights, expert_idx, down_weight):
@@ -514,6 +533,15 @@
             )
         )
     )
+    results = (act, logit, down)
+    act, logit, down = pl.pallas_call(
+        store_kernel,
+        out_shape=tuple(jax.ShapeDtypeStruct(of.shape, of.dtype) for of in results),
+        in_specs=[vmem] * 3,
+        out_specs=(hbm,) * 3,
+        scratch_shapes=[dma((3 * STRIPS,))],
+        compiler_params=pltpu.CompilerParams(vmem_limit_bytes=16 * 1024 * 1024),
+    )(*results)
     return act.reshape(tok, top, width), logit.T, down[None]
 
 

time: 43.6 us -> 43.4 us (level); the launches traced: 42.8 us -> 43.3 us
  Pallas kernels: 39.2 us -> 42.6 us
  local copies, waits for them, and re-layouts: 2.94 us -> 0 us
    unnamed x3 -> x0, local copies, waits for them, and re-layouts: 2.94 us -> none
    pallas_call x0 -> x1, Pallas kernels: none -> 1.83 us  [gathered_shards(): pl.pallas_call(store_kernel, out_shape=tuple((jax.ShapeDtypeStruct(of.sha...]
    pallas_call x1, Pallas kernels: 39.2 us -> 40.8 us  [gathered_shards(): pl.pallas_call(gather_kernel, out_shape=(jax.ShapeDtypeStruct((tok * top,...]
where the time goes in v5:
time: 43.4 us; the launch traced here: 43.3 us
  Pallas kernels  42.6 us (98%)
  between operations  0.64 us (1%)
    pallas_call x1, Pallas kernels, gathered_shards(): pl.pallas_call(gather_kernel, out_shape=(jax.ShapeDtypeStruct((tok * top,...  40.8 us
    pallas_call x1, Pallas kernels, gathered_shards(): pl.pallas_call(store_kernel, out_shape=tuple((jax.ShapeDtypeStruct(of.sha...  1.83 us

profile of v5, /device:TPU:0, one launch (start us, length us, event | category | flops | bytes accessed | tf_op | source)
XLA Modules:
  0.0 43.3 jit_solution(4050666882854052139)
XLA Ops:
  0.6 40.8 %shard_map.76 = (bf16[128,768]{1,0:T(8,128)(2,1)S(1)}, f32[8,16]{1,0:T(8,128)S(1)}, bf16[384,4096]{1,0:T(8,128)(2,1)S(1)}) custom-call(f32[8,16]{1,0:T(8,128)} %bitcast.11, s32[8,16]{1,0:T(8,128)} %bitcast.12, bf16[128,768]{1,0:T(8,128)(2,1)} %bitcast.9, bf16[16,4096]{1,0:T(8,128)(2,1)} %grad_ref.1, bf16[768,4096]{1,0:T(8,128)(2,1)} %bitcast.7), custom_call_target="tpu_custom_call" | custom-call | flops 4831838208 | bytes 18874368 | tf_op jit(solution)/shard_map/pallas_call | solution.py:486
  41.5 1.8 %shard_map.77 = (bf16[128,768]{1,0:T(8,128)(2,1)}, f32[8,16]{1,0:T(8,128)}, bf16[384,4096]{1,0:T(8,128)(2,1)}) custom-call(bf16[128,768]{1,0:T(8,128)(2,1)S(1)} %get-tuple-element.9.refs_0_, f32[8,16]{1,0:T(8,128)S(1)} %get-tuple-element.10.refs_1_, bf16[384,4096]{1,0:T(8,128)(2,1)S(1)} %get-tuple-element.11.refs_2_), custom_call_target="tpu_custom_call" | custom-call | tf_op jit(solution)/shard_map/pallas_call | solution.py:537

commit v6 on v5

--- a/solution.py
+++ b/solution.py
@@ -293,29 +293,40 @@
     def from_group(p, xx, dist):
         receive(p, 1 - y, xx, dist, False, xx is x and dist == 2, False)
 
-    def acts_copy(r):
-        other = lax.rem(lid + r, n_dev)
-        yy, ee = lax.div(other, n_exp), lax.rem(other, n_exp)
+    per_half = n_exp // 2
+    my_half = lax.div(me, per_half)
+
+    def far_exp(r):
+        return (1 - my_half) * per_half + lax.rem(me + r, per_half)
+
+    def near_exp(r):
+        return my_half * per_half + lax.rem(me + r, per_half)
+
+    def acts_copy(yy, ee):
         return pltpu.make_async_remote_copy(
             src_ref=acts_send.at[yy, ee], dst_ref=acts_in.at[own],
-            send_sem=h_send.at[r], recv_sem=h_recv.at[own],
+            send_sem=h_send.at[yy, ee], recv_sem=h_recv.at[own],
             device_id=dev(yy, ee), device_id_type=MESH,
         )
 
-    def acts_start(r, carry):
-        acts_copy(r).start()
+    def acts_far(r, carry):
+        acts_copy(y, far_exp(r)).start()
+        acts_copy(1 - y, far_exp(r)).start()
         return carry
 
+    def acts_near(r, group):
+        acts_copy(group, near_exp(r)).start()
+        return group
+
     own_acts = pltpu.make_async_copy(acts_send.at[y, me], acts_in.at[own], own_sem.at[1])
 
-    def back_copy(slot, zz, xx, cc):
+    def back_copy(ee):
+        at = slot_of(0, lax.rem(lax.div(ee, CS), XS), lax.div(ee, XS * CS), lax.rem(ee, CS))
         return pltpu.make_async_remote_copy(
-            src_ref=hid.at[slot], dst_ref=back.at[me],
-            send_sem=b_send.at[slot], recv_sem=b_recv.at[me],
-            device_id=dev(y, expert_of(xx, zz, cc)), device_id_type=MESH,
-        )
-
-    per_x = ZS * CS
+            src_ref=hid.at[at], dst_ref=back.at[me], send_sem=b_send.at[at],
+            recv_sem=b_recv.at[me], device_id=dev(y, ee), device_id_type=MESH,
+        )
+
     tile = model // 4
 
     def hidden(p):
@@ -341,6 +352,7 @@
         from_z(p, 1)
     for p in parts:
         from_x(p, 0)
+    lax.fori_loop(0, per_half, acts_far, 0)
     for p in parts:
         from_z(p, 2)
     for p in parts:
@@ -349,7 +361,8 @@
         from_z(p, 3)
     for p in parts:
         from_x(p, 2)
-    lax.fori_loop(1, n_dev, acts_start, 0)
+    lax.fori_loop(1, per_half, acts_near, y)
+    lax.fori_loop(0, per_half, acts_near, 1 - y)
     own_acts.start()
     for dist in range(2):
         for p in parts:
@@ -362,15 +375,10 @@
     own_back = pltpu.make_async_copy(hid.at[own - y * n_exp], back.at[me], own_sem.at[0])
     own_back.start()
 
-    def each_back():
-        for xx in (1 - x, x):
-            for r in range(per_x):
-                at = lax.rem(z * CS + c + r, per_x)
-                if xx is not x or r:
-                    yield back_copy(xx * per_x + at, lax.div(at, CS), xx, lax.rem(at, CS))
-
-    for copy in each_back():
-        copy.start()
+    for r in range(per_half):
+        back_copy(far_exp(r)).start()
+    for r in range(1, per_half):
+        back_copy(near_exp(r)).start()
 
     def acts_wait(r, group):
         ee = lax.rem(me + r, n_exp)
@@ -379,7 +387,7 @@
         )
         pltpu.make_async_remote_copy(
             src_ref=acts_send.at[0, 0], dst_ref=acts_in.at[slot],
-            send_sem=h_send.at[0], recv_sem=h_recv.at[slot],
+            send_sem=h_send.at[0, 0], recv_sem=h_recv.at[slot],
             device_id=dev(1 - y, me), device_id_type=MESH,
         ).wait_recv()
         return group
@@ -429,13 +437,14 @@
         else:
             pl.when(when)(copy.wait_send)
 
-    def acts_sent(r, carry):
-        acts_copy(r).wait_send()
-        return carry
-
-    lax.fori_loop(1, n_dev, acts_sent, 0)
-    for copy in each_back():
-        copy.wait_send()
+    def acts_sent(r, group):
+        acts_copy(group, lax.rem(me + r, n_exp)).wait_send()
+        return group
+
+    lax.fori_loop(1, n_exp, acts_sent, y)
+    lax.fori_loop(0, n_exp, acts_sent, 1 - y)
+    for r in range(1, n_exp):
+        back_copy(lax.rem(me + r, n_exp)).wait_send()
 
     def back_wait(r, carry):
         ee = lax.rem(me + r, n_exp)
@@ -512,7 +521,7 @@
             dma((PARTS, ZS + 1)),
             dma((PARTS, XS * ZS)),
             dma((PARTS, 2 * XS * ZS)),
-            dma((n_dev,)),
+            dma((2, n_exp)),
             dma((n_dev,)),
             dma((n_exp,)),
             dma((n_exp,)),

time: 43.4 us -> 48.3 us (1.11)
  Pallas kernels: 42.6 us -> 47.5 us
    pallas_call x1, Pallas kernels: 40.8 us -> 45.7 us  [gathered_shards(): pl.pallas_call(gather_kernel, out_shape=(jax.ShapeDtypeStruct((tok * top,...]
where the time goes in v6:
time: 48.3 us; the launch traced here: 48.1 us
  Pallas kernels  47.5 us (98%)
  between operations  0.64 us (1%)
    pallas_call x1, Pallas kernels, gathered_shards(): pl.pallas_call(gather_kernel, out_shape=(jax.ShapeDtypeStruct((tok * top,...  45.7 us
    pallas_call x1, Pallas kernels, gathered_shards(): pl.pallas_call(store_kernel, out_shape=tuple((jax.ShapeDtypeStruct(of.sha...  1.83 us

profile of v6, /device:TPU:0, one launch (start us, length us, event | category | flops | bytes accessed | tf_op | source)
XLA Modules:
  0.0 48.1 jit_solution(13702752708092221004)
XLA Ops:
  0.6 45.7 %shard_map.76 = (bf16[128,768]{1,0:T(8,128)(2,1)S(1)}, f32[8,16]{1,0:T(8,128)S(1)}, bf16[384,4096]{1,0:T(8,128)(2,1)S(1)}) custom-call(f32[8,16]{1,0:T(8,128)} %bitcast.11, s32[8,16]{1,0:T(8,128)} %bitcast.12, bf16[128,768]{1,0:T(8,128)(2,1)} %bitcast.9, bf16[16,4096]{1,0:T(8,128)(2,1)} %grad_ref.1, bf16[768,4096]{1,0:T(8,128)(2,1)} %bitcast.7), custom_call_target="tpu_custom_call" | custom-call | flops 4831838208 | bytes 18874368 | tf_op jit(solution)/shard_map/pallas_call | solution.py:495
  46.3 1.8 %shard_map.77 = (bf16[128,768]{1,0:T(8,128)(2,1)}, f32[8,16]{1,0:T(8,128)}, bf16[384,4096]{1,0:T(8,128)(2,1)}) custom-call(bf16[128,768]{1,0:T(8,128)(2,1)S(1)} %get-tuple-element.9.refs_0_, f32[8,16]{1,0:T(8,128)S(1)} %get-tuple-element.10.refs_1_, bf16[384,4096]{1,0:T(8,128)(2,1)S(1)} %get-tuple-element.11.refs_2_), custom_call_target="tpu_custom_call" | custom-call | tf_op jit(solution)/shard_map/pallas_call | solution.py:546

commit v7 on v6

--- a/solution.py
+++ b/solution.py
@@ -202,10 +202,10 @@
         if to_x:
             at = zz if yy is y else ZS
             send(grad_copy(p, slot, x_send.at[p, at], y, expert_of(1 - x, z, c)), when)
+        at = yy * XS * ZS + in_plane
+        send(grad_copy(p, slot, c_send.at[p, at], y, expert_of(x, z, 1 - c)), when)
         if to_y:
             send(grad_copy(p, slot, y_send.at[p, in_plane], 1 - y, me), when)
-        at = yy * XS * ZS + in_plane
-        send(grad_copy(p, slot, c_send.at[p, at], y, expert_of(x, z, 1 - c)), when)
 
     def along_z(p, zz, way, when):
         slot = slot_of(y, x, zz, c)
@@ -293,15 +293,6 @@
     def from_group(p, xx, dist):
         receive(p, 1 - y, xx, dist, False, xx is x and dist == 2, False)
 
-    per_half = n_exp // 2
-    my_half = lax.div(me, per_half)
-
-    def far_exp(r):
-        return (1 - my_half) * per_half + lax.rem(me + r, per_half)
-
-    def near_exp(r):
-        return my_half * per_half + lax.rem(me + r, per_half)
-
     def acts_copy(yy, ee):
         return pltpu.make_async_remote_copy(
             src_ref=acts_send.at[yy, ee], dst_ref=acts_in.at[own],
@@ -309,14 +300,28 @@
             device_id=dev(yy, ee), device_id_type=MESH,
         )
 
-    def acts_far(r, carry):
-        acts_copy(y, far_exp(r)).start()
-        acts_copy(1 - y, far_exp(r)).start()
+    inner = (z > 0) & (z < ZS - 1)
+    per_z = XS * CS
+
+    def acts_early(r, carry):
+        ee = (ZS - 1 - z) * per_z + lax.rem(me + r, per_z)
+        acts_copy(y, ee).start()
+        acts_copy(1 - y, ee).start()
         return carry
 
-    def acts_near(r, group):
-        acts_copy(group, near_exp(r)).start()
-        return group
+    def acts_late(r, carry):
+        ee = lax.rem(me + r, n_exp)
+        waits = jnp.logical_not(inner & (lax.div(ee, per_z) == ZS - 1 - z))
+
+        @pl.when(waits & (r > 0))
+        def _():
+            acts_copy(y, ee).start()
+
+        @pl.when(waits)
+        def _():
+            acts_copy(1 - y, ee).start()
+
+        return carry
 
     own_acts = pltpu.make_async_copy(acts_send.at[y, me], acts_in.at[own], own_sem.at[1])
 
@@ -352,7 +357,11 @@
         from_z(p, 1)
     for p in parts:
         from_x(p, 0)
-    lax.fori_loop(0, per_half, acts_far, 0)
+
+    @pl.when(inner)
+    def _():
+        lax.fori_loop(0, per_z, acts_early, 0)
+
     for p in parts:
         from_z(p, 2)
     for p in parts:
@@ -361,8 +370,7 @@
         from_z(p, 3)
     for p in parts:
         from_x(p, 2)
-    lax.fori_loop(1, per_half, acts_near, y)
-    lax.fori_loop(0, per_half, acts_near, 1 - y)
+    lax.fori_loop(0, n_exp, acts_late, 0)
     own_acts.start()
     for dist in range(2):
         for p in parts:
@@ -375,10 +383,8 @@
     own_back = pltpu.make_async_copy(hid.at[own - y * n_exp], back.at[me], own_sem.at[0])
     own_back.start()
 
-    for r in range(per_half):
-        back_copy(far_exp(r)).start()
-    for r in range(1, per_half):
-        back_copy(near_exp(r)).start()
+    for r in range(1, n_exp):
+        back_copy(lax.rem(me + r, n_exp)).start()
 
     def acts_wait(r, group):
         ee = lax.rem(me + r, n_exp)

time: 48.3 us -> 44 us (0.911)
  Pallas kernels: 47.5 us -> 43.3 us
    pallas_call x1, Pallas kernels: 45.7 us -> 41.4 us  [gathered_shards(): pl.pallas_call(gather_kernel, out_shape=(jax.ShapeDtypeStruct((tok * top,...]
where the time goes in v7:
time: 44 us; the launch traced here: 43.9 us
  Pallas kernels  43.3 us (98%)
  between operations  0.64 us (1%)
    pallas_call x1, Pallas kernels, gathered_shards(): pl.pallas_call(gather_kernel, out_shape=(jax.ShapeDtypeStruct((tok * top,...  41.4 us
    pallas_call x1, Pallas kernels, gathered_shards(): pl.pallas_call(store_kernel, out_shape=tuple((jax.ShapeDtypeStruct(of.sha...  1.83 us

profile of v7, /device:TPU:0, one launch (start us, length us, event | category | flops | bytes accessed | tf_op | source)
XLA Modules:
  0.0 43.9 jit_solution(759563789340237906)
XLA Ops:
  0.6 41.4 %shard_map.76 = (bf16[128,768]{1,0:T(8,128)(2,1)S(1)}, f32[8,16]{1,0:T(8,128)S(1)}, bf16[384,4096]{1,0:T(8,128)(2,1)S(1)}) custom-call(f32[8,16]{1,0:T(8,128)} %bitcast.11, s32[8,16]{1,0:T(8,128)} %bitcast.12, bf16[128,768]{1,0:T(8,128)(2,1)} %bitcast.9, bf16[16,4096]{1,0:T(8,128)(2,1)} %grad_ref.1, bf16[768,4096]{1,0:T(8,128)(2,1)} %bitcast.7), custom_call_target="tpu_custom_call" | custom-call | flops 4831838208 | bytes 18874368 | tf_op jit(solution)/shard_map/pallas_call | solution.py:501
  42.1 1.8 %shard_map.77 = (bf16[128,768]{1,0:T(8,128)(2,1)}, f32[8,16]{1,0:T(8,128)}, bf16[384,4096]{1,0:T(8,128)(2,1)}) custom-call(bf16[128,768]{1,0:T(8,128)(2,1)S(1)} %get-tuple-element.9.refs_0_, f32[8,16]{1,0:T(8,128)S(1)} %get-tuple-element.10.refs_1_, bf16[384,4096]{1,0:T(8,128)(2,1)S(1)} %get-tuple-element.11.refs_2_), custom_call_target="tpu_custom_call" | custom-call | tf_op jit(solution)/shard_map/pallas_call | solution.py:552

commit v8 on v5

--- a/solution.py
+++ b/solution.py
@@ -347,10 +347,10 @@
         from_x(p, 1)
     for p in parts:
         from_z(p, 3)
-    for p in parts:
-        from_x(p, 2)
     lax.fori_loop(1, n_dev, acts_start, 0)
     own_acts.start()
+    for p in parts:
+        from_x(p, 2)
     for dist in range(2):
         for p in parts:
             from_group(p, x, dist)
@@ -400,10 +400,6 @@
         for p in parts:
             from_group(p, x, dist)
 
-    for dist in range(ZS):
-        for p in parts:
-            from_group(p, 1 - x, dist)
-
     lax.fori_loop(1, n_exp, acts_wait, y)
     own_acts.wait()
     turn(y, 0)
@@ -413,6 +409,10 @@
         cols = pl.ds(pl.multiple_of(n * tile, tile), tile)
         total[:, cols] = down_part(y, 0, n)
 
+    for dist in range(ZS):
+        for p in parts:
+            from_group(p, 1 - x, dist)
+
     lax.fori_loop(0, n_exp, acts_wait, 1 - y)
     turn(1 - y, 1)
     for p in parts:
@@ -422,20 +422,6 @@
     def _(n):
         cols = pl.ds(pl.multiple_of(n * tile, tile), tile)
         down_out[:, cols] = (total[:, cols] + down_part(1 - y, 1, n)).astype(jnp.bfloat16)
-
-    for when, copy in sent:
-        if when is None:
-            copy.wait_send()
-        else:
-            pl.when(when)(copy.wait_send)
-
-    def acts_sent(r, carry):
-        acts_copy(r).wait_send()
-        return carry
-
-    lax.fori_loop(1, n_dev, acts_sent, 0)
-    for copy in each_back():
-        copy.wait_send()
 
     def back_wait(r, carry):
         ee = lax.rem(me + r, n_exp)
@@ -454,6 +440,20 @@
     score = score.astype(jnp.bfloat16).astype(jnp.float32)
     score = jnp.dot(own_row.astype(jnp.float32), score * spread, preferred_element_type=jnp.float32)
     logit_out[...] = gate * (score - jnp.sum(gate * score, axis=0, keepdims=True))
+
+    for when, copy in sent:
+        if when is None:
+            copy.wait_send()
+        else:
+            pl.when(when)(copy.wait_send)
+
+    def acts_sent(r, carry):
+        acts_copy(r).wait_send()
+        return carry
+
+    lax.fori_loop(1, n_dev, acts_sent, 0)
+    for copy in each_back():
+        copy.wait_send()
 
 
 def store_kernel(*refs):

time: 43.4 us -> 42.5 us (0.979); the launches traced: 43.3 us -> 41.7 us
  Pallas kernels: 42.6 us -> 41 us
    pallas_call x1, Pallas kernels: 40.8 us -> 39.2 us  [gathered_shards(): pl.pallas_call(gather_kernel, out_shape=(jax.ShapeDtypeStruct((tok * top,...]
where the time goes in v8:
time: 42.5 us; the launch traced here: 41.7 us
  Pallas kernels  41 us (96%)
  between operations  0.64 us (2%)
    pallas_call x1, Pallas kernels, gathered_shards(): pl.pallas_call(gather_kernel, out_shape=(jax.ShapeDtypeStruct((tok * top,...  39.2 us
    pallas_call x1, Pallas kernels, gathered_shards(): pl.pallas_call(store_kernel, out_shape=tuple((jax.ShapeDtypeStruct(of.sha...  1.83 us

profile of v8, /device:TPU:0, one launch (start us, length us, event | category | flops | bytes accessed | tf_op | source)
XLA Modules:
  0.0 41.7 jit_solution(3425566253011458913)
XLA Ops:
  0.6 39.2 %shard_map.76 = (bf16[128,768]{1,0:T(8,128)(2,1)S(1)}, f32[8,16]{1,0:T(8,128)S(1)}, bf16[384,4096]{1,0:T(8,128)(2,1)S(1)}) custom-call(f32[8,16]{1,0:T(8,128)} %bitcast.11, s32[8,16]{1,0:T(8,128)} %bitcast.12, bf16[128,768]{1,0:T(8,128)(2,1)} %bitcast.9, bf16[16,4096]{1,0:T(8,128)(2,1)} %grad_ref.1, bf16[768,4096]{1,0:T(8,128)(2,1)} %bitcast.7), custom_call_target="tpu_custom_call" | custom-call | flops 4831838208 | bytes 18874368 | tf_op jit(solution)/shard_map/pallas_call | solution.py:486
  39.8 1.8 %shard_map.77 = (bf16[128,768]{1,0:T(8,128)(2,1)}, f32[8,16]{1,0:T(8,128)}, bf16[384,4096]{1,0:T(8,128)(2,1)}) custom-call(bf16[128,768]{1,0:T(8,128)(2,1)S(1)} %get-tuple-element.9.refs_0_, f32[8,16]{1,0:T(8,128)S(1)} %get-tuple-element.10.refs_1_, bf16[384,4096]{1,0:T(8,128)(2,1)S(1)} %get-tuple-element.11.refs_2_), custom_call_target="tpu_custom_call" | custom-call | tf_op jit(solution)/shard_map/pallas_call | solution.py:537
